TPU v7x, 512 devices: a whole 4x8x8 slice. The times are simulated.
512 devices in a mesh: seq: 64 (over z_lo, y, core), dp: 8 (over z_hi, x).
Axes of the slice: x: 4, y: 8, z: 8 (z_hi: 2, z_lo: 4; z = z_hi * 4 + z_lo), core: 2. Of those that a mesh axis runs over, the one named last changes fastest.
Arguments:
- sequence_acts: bfloat16 [8, 768, 16384], P('dp', None, 'seq'), may hold values from -6 to 6
- taps: float32 [2, 768, 3], replicated, may hold values from -2.5 to 2.5
- dilations: int32 [2], replicated, may hold values from 1 to 8, as said below
- left_link: int32 [8, 64], P('dp'), may hold values from -1 to 63, as said below
- projection: bfloat16 [896, 768], P('dp'), may hold values from -0.21875 to 0.21875
- head_cotangent: bfloat16 [8, 896, 8192], P('dp', 'seq'), may hold values from -16 to 16
Outputs:
- input_grad: bfloat16 [8, 768, 16384], P('dp', None, 'seq')
- projection_grad: float32 [896, 768], P('seq')
- taps_grad: float32 [2, 768, 3], replicated
Inputs may be any that keep to these rules, and one draw needn't show every extreme that they name: `dilations`: the last block's dilation is 8. `left_link`: entry s is -1 or (s - 1) mod 64; entry 0 is never -1; each window has at least one -1.
All inputs are finite; a program needn't handle non-finite values.
Results may differ from a plain program's by a relative error of at most 0.0058.
Values may be sent and summed in bfloat16 or wider, within the bound.
A program may use at most 64 MiB of HBM per device.

v0:
```python
import math

import jax
import jax.numpy as jnp
from jax import lax
from jax.sharding import PartitionSpec as P

BLOCK_COUNT = 2
DILATION_LIMIT = 8


gelu_scale = 0.7978845608028654


def with_halo(shard, sides, width):
    for axis, dim in sides:
        devices, length = (lax.axis_size(axis), shard.shape[dim])
        up = [(i, (i + 1) % devices) for i in range(devices)]
        down = [(j, i) for i, j in up]
        last = lax.slice_in_dim(shard, length - width, length, axis=dim)
        leading = lax.slice_in_dim(shard, 0, width, axis=dim)
        before = lax.ppermute(last, axis, up)
        after = lax.ppermute(leading, axis, down)
        shard = jnp.concatenate([before, shard, after], axis=dim)
    return shard


def gelu_result(v):
    inner = jnp.tanh(gelu_scale * (v + 0.044715 * v * v * v))
    return 0.5 * v * (1.0 + inner)


def gelu_slope(v):
    inner = jnp.tanh(gelu_scale * (v + 0.044715 * v * v * v))
    return 0.5 * (1.0 + inner) + 0.5 * v * (1.0 - inner * inner) * gelu_scale * (
        1.0 + 3.0 * 0.044715 * v * v
    )


def zero_border_rows(extended_rows, margin, left_linked, right_linked):
    columns = jnp.arange(extended_rows.shape[1])
    keep = ((columns >= margin) | left_linked) & (
        (columns < extended_rows.shape[1] - margin) | right_linked
    )
    return jnp.where(keep[None, :], extended_rows, jnp.zeros_like(extended_rows))


def tap_sum(extended_rows, weights, dilation, length, sign):
    margin = (extended_rows.shape[1] - length) // 2
    total = jnp.zeros((extended_rows.shape[0], length), jnp.float32)
    for tap_index in range(3):
        start_offset = margin + sign * (tap_index - 1) * dilation
        total = total + weights[:, tap_index][:, None] * lax.dynamic_slice_in_dim(
            extended_rows, start_offset, length, 1
        )
    return total


def local(sequence_acts, taps, dilations, left_link, projection, head_cotangent):
    x_start = sequence_acts[0]
    link = left_link[0]
    rows = x_start.shape[1]
    n_seq = lax.axis_size("seq")
    shard = lax.axis_index("seq")
    left_linked = lax.dynamic_index_in_dim(link, shard, keepdims=False) >= 0
    right_linked = lax.dynamic_index_in_dim(link, (shard + 1) % n_seq, keepdims=False) >= 0
    inputs = []
    acts = []
    running_state = x_start
    for block_number in range(BLOCK_COUNT):
        inputs.append(running_state)
        extended_rows = with_halo(running_state, (("seq", 1),), DILATION_LIMIT)
        block_activation = gelu_result(
            zero_border_rows(extended_rows, DILATION_LIMIT, left_linked, right_linked).astype(
                jnp.float32
            )
        )
        acts.append(block_activation)
        mixed = tap_sum(block_activation, taps[block_number], dilations[block_number], rows, 1)
        running_state = (running_state.astype(jnp.float32) + mixed).astype(jnp.bfloat16)
    pooled = (
        0.5
        * (running_state[:, 0::2].astype(jnp.float32) + running_state[:, 1::2].astype(jnp.float32))
    ).astype(jnp.bfloat16)
    regrouped = lax.all_to_all(head_cotangent, "seq", split_axis=2, concat_axis=1, tiled=True)
    cotangent = regrouped[0]
    back_pool = lax.dot_general(
        lax.all_gather(projection, "dp", axis=0, tiled=True),
        cotangent,
        (((0,), (0,)), ((), ())),
        preferred_element_type=jnp.float32,
    )
    running_gradient = jnp.repeat((0.5 * back_pool).astype(jnp.bfloat16), 2, axis=1)
    tap_grads = [None] * BLOCK_COUNT
    for block_number in reversed(range(BLOCK_COUNT)):
        extended_rows = with_halo(running_gradient, (("seq", 1),), DILATION_LIMIT)
        extended_rows = zero_border_rows(
            extended_rows, DILATION_LIMIT, left_linked, right_linked
        ).astype(jnp.float32)
        back = tap_sum(extended_rows, taps[block_number], dilations[block_number], rows, -1)
        grad_f = running_gradient.astype(jnp.float32)
        columns = []
        for tap_index in range(3):
            start_offset = DILATION_LIMIT + (tap_index - 1) * dilations[block_number]
            shifted = lax.dynamic_slice_in_dim(acts[block_number], start_offset, rows, 1)
            columns.append(jnp.sum(grad_f * shifted, axis=1))
        tap_grads[block_number] = jnp.stack(columns, axis=1)
        running_gradient = (
            grad_f + back * gelu_slope(inputs[block_number].astype(jnp.float32))
        ).astype(jnp.bfloat16)
    local_taps = jnp.stack(tap_grads, axis=0)
    share = cotangent.shape[0] // n_seq
    scale = 1.0 / math.sqrt(lax.axis_size("dp") * n_seq * pooled.shape[1])
    local_weight = lax.dot_general(
        cotangent, pooled, (((1,), (1,)), ((), ())), preferred_element_type=jnp.float32
    )
    weight_total, taps_total = lax.psum((local_weight, local_taps), ("seq", "dp"))
    weight_rows = lax.dynamic_slice_in_dim(weight_total, shard * share, share, 0)
    return (running_gradient[None], weight_rows * scale, taps_total * scale)


def solution(mesh):
    placed = (P("dp", None, "seq"), P(), P(), P("dp", None), P("dp", None), P("dp", "seq", None))
    return jax.shard_map(
        local,
        mesh=mesh,
        in_specs=placed,
        out_specs=(P("dp", None, "seq"), P("seq", None), P()),
        check_vma=False,
    )
```

profile of v0, /device:TPU:1, one launch (start us, length us, event | category | flops | bytes accessed | tf_op | source)
XLA Modules:
  0.0 455.4 jit_solution(7650657632617837215)
XLA Ops:
  7.9 8.4 %copy.27 = bf16[1,14,8192]{1,0,2:T(2,128)(2,1)} copy(bf16[1,14,8192]{2,1,0:T(8,128)(2,1)} %param.11) | data formatting | bytes 458752 | tf_op args[5]
  16.8 45.2 %reduce.12 = bf16[8192,14]{1,0:T(8,128)(2,1)S(1)} reduce(bf16[8192,1,14]{2,1,0:T(2,128)(2,1)} %bitcast.41, bf16[]{:T(256)} %broadcast.119), dimensions={1}, to_apply=%bitcast.35.reduce_sub_computation | reduce | bytes 458754
  62.0 4.4 reshape.54
  66.5 14.7 %all-to-all-start = ((bf16[64,2,896]{2,1,0:T(2,128)(2,1)}), bf16[64,2,896]{2,1,0:T(2,128)(2,1)S(1)}, u32[]{:S(2)}, u32[]{:S(2)}) async-start(bf16[64,2,896]{2,1,0:T(2,128)(2,1)} %reshape.54), calls=%async_computation | async-start | bytes 458752 | tf_op jit(solution)/shard_map/all_to_all | solution.py:85
  81.4 3.5 collective-permute-start.2
  84.9 1.9 collective-permute-start.3
  93.4 8.1 %reshape.55 = bf16[8192,1,14]{2,1,0:T(2,128)(2,1)} reshape(bf16[64,2,896]{2,1,0:T(2,128)(2,1)S(1)} %all-to-all-done) | data formatting | bytes 458752
  101.6 8.1 %copy.28 = bf16[1,14,8192]{2,1,0:T(8,128)(2,1)S(1)} copy(bf16[1,14,8192]{1,0,2:T(2,128)(2,1)} %bitcast.42) | data formatting | bytes 458752 | tf_op jit(solution)/shard_map/all_to_all | solution.py:85
  110.1 1.9 fusion.8
  112.8 3.6 collective-permute-start
  116.4 4.8 %collective-permute-start.1 = (bf16[768,8]{1,0:T(8,128)(2,1)S(1)}, bf16[768,8]{1,0:T(8,128)(2,1)S(1)}, u32[]{:S(2)}, u32[]{:S(2)}) collective-permute-start(bf16[768,8]{1,0:T(8,128)(2,1)S(1)} %get-tuple-element.35), channel_id=1, source_target_pairs={{8,0},{16,8},{24,16},{32,24},{40,32},{48,40},{56,48},{64,56},{72,6... | collective-permute-start | bytes 36872 | tf_op jit(solution)/shard_map/ppermute | solution.py:23
  122.0 1.5 collective-permute-done.1
  123.8 2.7 fusion.14
  126.6 1.9 collective-permute-start.6
  128.6 8.4 %collective-permute-start.7 = (bf16[768,8]{1,0:T(8,128)(2,1)S(1)}, bf16[768,8]{1,0:T(8,128)(2,1)S(1)}, u32[]{:S(2)}, u32[]{:S(2)}) collective-permute-start(bf16[768,8]{1,0:T(8,128)(2,1)S(1)} %get-tuple-element.31), channel_id=1, source_target_pairs={{8,0},{16,8},{24,16},{32,24},{40,32},{48,40},{56,48},{64,56},{72,6... | collective-permute-start | bytes 36872 | tf_op jit(solution)/shard_map/ppermute | solution.py:23
  138.6 1.5 fusion.10
  140.2 8.2 %slice.92 = bf16[768,128]{1,0:T(8,128)(2,1)S(1)} slice(bf16[768,256]{1,0:T(8,128)(2,1)S(1)} %get-tuple-element.29), slice={[0:768:1], [0:256:2]} | slice | bytes 393216 | tf_op jit(solution)/shard_map/slice | solution.py:83
  148.4 8.2 %slice.93 = bf16[768,128]{1,0:T(8,128)(2,1)S(1)} slice(bf16[768,256]{1,0:T(8,128)(2,1)S(1)} %get-tuple-element.29), slice={[0:768:1], [1:256:2]} | slice | bytes 393216 | tf_op jit(solution)/shard_map/slice | solution.py:83
  156.6 2.1 convolution_bitcast_fusion
  158.9 1.9 collective-permute-start.4
  160.8 9.8 %collective-permute-start.5 = (bf16[768,8]{1,0:T(8,128)(2,1)S(1)}, bf16[768,8]{1,0:T(8,128)(2,1)S(1)}, u32[]{:S(2)}, u32[]{:S(2)}) collective-permute-start(bf16[768,8]{1,0:T(8,128)(2,1)S(1)} %get-tuple-element.33), channel_id=1, source_target_pairs={{8,0},{16,8},{24,16},{32,24},{40,32},{48,40},{56,48},{64,56},{72,6... | collective-permute-start | bytes 36872 | tf_op jit(solution)/shard_map/ppermute | solution.py:23
  170.8 104.9 %psum.15 = f32[2,768,3]{1,2,0:T(4,128)S(1)} all-reduce(f32[2,768,3]{1,2,0:T(4,128)S(1)} %pad_maximum_fusion), channel_id=1, replica_groups=mesh['seq'=64,'dp'=8] {'seq','dp'}, use_global_device_ids=true, to_apply=%region_7.8 | all-reduce | flops 4608 | bytes 36864 | tf_op jit(solution)/shard_map/psum | solution.py:117
  276.7 1.9 fusion.41
  278.6 167.9 %all-reduce.2.cloned.1.call-done = f32[896,768]{0,1:T(8,128)} async-done(((f32[896,768]{0,1:T(8,128)}), f32[896,768]{0,1:T(8,128)}) %all-reduce.2.cloned.1.call-update) | async-done | bytes 2752528 | tf_op jit(solution)/shard_map/psum | solution.py:117
  (58 shorter events, 9.9 us)
Async XLA Ops:
  7.2 102.9 %all-gather.2.cloned.1.call-start = ((), (), s32[]{:S(2)}) async-start(), calls=%async_computation.1 | async-start | bytes 1548288 | tf_op jit(solution)/shard_map/all_gather | solution.py:88
  62.0 19.2 %copy-start = (bf16[1,768,256]{2,1,0:T(8,128)(2,1)S(1)}, bf16[1,768,256]{2,1,0:T(8,128)(2,1)}, u32[]{:S(2)}) copy-start(bf16[1,768,256]{2,1,0:T(8,128)(2,1)} %param.6) | copy-start | bytes 1179652
  66.4 20.4 %copy-start.3 = (s32[2]{0:T(128)S(1)}, s32[2]{0:T(128)}, u32[]{:S(2)}) copy-start(s32[2]{0:T(128)} %param.8) | copy-start | bytes 28
  66.4 24.9 %copy-start.2 = (s32[1,64]{1,0:T(1,128)S(1)}, s32[1,64]{1,0:T(1,128)}, u32[]{:S(2)}) copy-start(s32[1,64]{1,0:T(1,128)} %param.9) | copy-start | bytes 772
  66.5 26.8 %copy-start.1 = (f32[2,768,3]{1,0,2:T(2,128)S(1)}, f32[2,768,3]{1,0,2:T(2,128)}, u32[]{:S(2)}) copy-start(f32[2,768,3]{1,0,2:T(2,128)} %param.7) | copy-start | bytes 55300
  66.5 27.0 %all-to-all-start = ((bf16[64,2,896]{2,1,0:T(2,128)(2,1)}), bf16[64,2,896]{2,1,0:T(2,128)(2,1)S(1)}, u32[]{:S(2)}, u32[]{:S(2)}) async-start(bf16[64,2,896]{2,1,0:T(2,128)(2,1)} %reshape.54), calls=%async_computation | async-start | bytes 458752 | tf_op jit(solution)/shard_map/all_to_all | solution.py:85
  81.2 365.3 %all-reduce.2.cloned.1.call-start = ((), (), s32[]{:S(2)}) async-start(), calls=%async_computation.2 | async-start | bytes 5505024 | tf_op jit(solution)/shard_map/psum | solution.py:117
  81.4 39.9 %collective-permute-start.2 = (bf16[768,8]{1,0:T(8,128)(2,1)S(1)}, bf16[768,8]{1,0:T(8,128)(2,1)S(1)}, u32[]{:S(2)}, u32[]{:S(2)}) collective-permute-start(bf16[768,8]{1,0:T(8,128)(2,1)S(1)} %get-tuple-element.36), channel_id=1, source_target_pairs={{0,8},{8,16},{16,24},{24,32},{32,40},{40,48},{48,56},{56,64},{64,7... | collective-permute-start | bytes 36872 | tf_op jit(solution)/shard_map/ppermute | solution.py:22
  84.9 36.4 %collective-permute-start.3 = (bf16[768,8]{1,0:T(8,128)(2,1)S(1)}, bf16[768,8]{1,0:T(8,128)(2,1)S(1)}, u32[]{:S(2)}, u32[]{:S(2)}) collective-permute-start(bf16[768,8]{1,0:T(8,128)(2,1)S(1)} %get-tuple-element.37), channel_id=1, source_target_pairs={{8,0},{16,8},{24,16},{32,24},{40,32},{48,40},{56,48},{64,56},{72,6... | collective-permute-start | bytes 36872 | tf_op jit(solution)/shard_map/ppermute | solution.py:23
  112.8 9.2 %collective-permute-start = (bf16[768,8]{1,0:T(8,128)(2,1)S(1)}, bf16[768,8]{1,0:T(8,128)(2,1)S(1)}, u32[]{:S(2)}, u32[]{:S(2)}) collective-permute-start(bf16[768,8]{1,0:T(8,128)(2,1)S(1)} %get-tuple-element.34), channel_id=1, source_target_pairs={{0,8},{8,16},{16,24},{24,32},{32,40},{40,48},{48,56},{56,64},{64,7... | collective-permute-start | bytes 36872 | tf_op jit(solution)/shard_map/ppermute | solution.py:22
  116.4 7.0 %collective-permute-start.1 = (bf16[768,8]{1,0:T(8,128)(2,1)S(1)}, bf16[768,8]{1,0:T(8,128)(2,1)S(1)}, u32[]{:S(2)}, u32[]{:S(2)}) collective-permute-start(bf16[768,8]{1,0:T(8,128)(2,1)S(1)} %get-tuple-element.35), channel_id=1, source_target_pairs={{8,0},{16,8},{24,16},{32,24},{40,32},{48,40},{56,48},{64,56},{72,6... | collective-permute-start | bytes 36872 | tf_op jit(solution)/shard_map/ppermute | solution.py:23
  126.6 10.3 %collective-permute-start.6 = (bf16[768,8]{1,0:T(8,128)(2,1)S(1)}, bf16[768,8]{1,0:T(8,128)(2,1)S(1)}, u32[]{:S(2)}, u32[]{:S(2)}) collective-permute-start(bf16[768,8]{1,0:T(8,128)(2,1)S(1)} %get-tuple-element.30), channel_id=1, source_target_pairs={{0,8},{8,16},{16,24},{24,32},{32,40},{40,48},{48,56},{56,64},{64,7... | collective-permute-start | bytes 36872 | tf_op jit(solution)/shard_map/ppermute | solution.py:22
  128.6 9.4 %collective-permute-start.7 = (bf16[768,8]{1,0:T(8,128)(2,1)S(1)}, bf16[768,8]{1,0:T(8,128)(2,1)S(1)}, u32[]{:S(2)}, u32[]{:S(2)}) collective-permute-start(bf16[768,8]{1,0:T(8,128)(2,1)S(1)} %get-tuple-element.31), channel_id=1, source_target_pairs={{8,0},{16,8},{24,16},{32,24},{40,32},{48,40},{56,48},{64,56},{72,6... | collective-permute-start | bytes 36872 | tf_op jit(solution)/shard_map/ppermute | solution.py:23
  158.9 117.4 %collective-permute-start.4 = (bf16[768,8]{1,0:T(8,128)(2,1)S(1)}, bf16[768,8]{1,0:T(8,128)(2,1)S(1)}, u32[]{:S(2)}, u32[]{:S(2)}) collective-permute-start(bf16[768,8]{1,0:T(8,128)(2,1)S(1)} %get-tuple-element.32), channel_id=1, source_target_pairs={{0,8},{8,16},{16,24},{24,32},{32,40},{40,48},{48,56},{56,64},{64,7... | collective-permute-start | bytes 36872 | tf_op jit(solution)/shard_map/ppermute | solution.py:22
  160.8 115.5 %collective-permute-start.5 = (bf16[768,8]{1,0:T(8,128)(2,1)S(1)}, bf16[768,8]{1,0:T(8,128)(2,1)S(1)}, u32[]{:S(2)}, u32[]{:S(2)}) collective-permute-start(bf16[768,8]{1,0:T(8,128)(2,1)S(1)} %get-tuple-element.33), channel_id=1, source_target_pairs={{8,0},{16,8},{24,16},{32,24},{40,32},{48,40},{56,48},{64,56},{72,6... | collective-permute-start | bytes 36872 | tf_op jit(solution)/shard_map/ppermute | solution.py:23
Sparse Core Ops, SparseCore 0:
  11.2 76.5 all-gather.1
  158.9 287.5 all-reduce.1
where the time goes:
time: 457 us; the launch traced here: 455 us
  waiting for transfers between devices  171 us (37%)
  blocking collectives  105 us (23%)
  other arithmetic  54.7 us (12%)
  starting transfers between devices  50.8 us (11%)
  local copies, waits for them, and re-layouts  50.2 us (11%)
  between operations  19.7 us (4%)
    psum x1, waiting for transfers between devices, local(): lax.psum((local_weight, local_taps), ('seq', 'dp'))  168 us
    psum x1, blocking collectives, local(): lax.psum((local_weight, local_taps), ('seq', 'dp'))  105 us
    unnamed x1, other arithmetic  45.2 us
    ppermute x4, starting transfers between devices, with_halo(): after = lax.ppermute(leading, axis, down)  25 us
    unnamed x16, local copies, waits for them, and re-layouts  22.9 us
    all_to_all x1, starting transfers between devices, local(): lax.all_to_all(head_cotangent, 'seq', split_axis=2, concat_axis=1, tiled=...  14.7 us
    ppermute x4, starting transfers between devices, with_halo(): before = lax.ppermute(last, axis, up)  11 us
  transfers between devices with their start and end apart: 11, of which 3 were waited for; matrix products, arithmetic and copies ran while one was open for 18% of the time, Pallas kernels for 0%

commit v1 on v0

v1 whole, which is shorter than its diff:
```python
import functools
import math

import jax
import jax.numpy as jnp
from jax import lax
from jax.experimental import pallas as pl
from jax.experimental.pallas import tpu as pltpu
from jax.sharding import PartitionSpec as P

MESH = pl.DeviceIdType.MESH
BF = jnp.bfloat16
F32 = jnp.float32

C = 768
ROWS = 256
HALF = 128
SEQ = 64
DP = 8
OWN = 14
PAD = 16
SLAB = 32
LAST_DILATION = 8
GELU = 0.7978845608028654


def gelu_pair(v):
    th = jnp.tanh(GELU * (v + 0.044715 * v * v * v))
    act = 0.5 * v * (1.0 + th)
    slope = 0.5 * (1.0 + th) + 0.5 * v * (1.0 - th * th) * GELU * (1.0 + 3.0 * 0.044715 * v * v)
    return act, slope


def rounded(v):
    return v.astype(BF).astype(F32)


def earlier(tiles, lane, d):
    turned = [pltpu.roll(t, d, 1) for t in tiles]
    return [jnp.where(lane < d, turned[j - 1], turned[j]) for j in range(len(tiles))]


def later(tiles, lane, d):
    turned = [pltpu.roll(t, HALF - d, 1) for t in tiles]
    n = len(tiles)
    return [jnp.where(lane >= HALF - d, turned[(j + 1) % n], turned[j]) for j in range(n)]


def kernel(
    x_ref, taps_ref, dil_ref, link_ref, proj_ref, cot_ref,
    out_ref, pg_ref, tg_ref,
    stage, cot, cot_sib, pfull, edge_s, edge_r, gedge_s, gedge_r, halo, wcol,
    a0, a1, s0, s1, x2, pooled, pooled_sib, g2, tcol,
    a_s1, a_r1, a_s2, a_r2, a_s3, a_r3, a_r4, b_s1, b_r1, b_s2, b_r2, b_r3,
    t_s, t_r1, t_r2, t_r3, t_f,
    send, recv,
):
    s = lax.axis_index("seq")
    d = lax.axis_index("dp")
    core = s % 2
    y = (s // 2) % 8
    zl = s // 16
    x = d % 4
    zh = d // 4
    z8 = zh * 4 + zl
    sib = s + 1 - 2 * core

    def at_x(k):
        return {"seq": s, "dp": zh * 4 + (x + k) % 4}

    def at_x_core(xx, cc):
        return {"seq": s - core + cc, "dp": zh * 4 + xx}

    def at_y(yy):
        return {"seq": zl * 16 + yy * 2 + core, "dp": d}

    def at_z(zz):
        return {"seq": (zz % 4) * 16 + y * 2 + core, "dp": (zz // 4) * 4 + x}

    def push(src, dst, i, where):
        pltpu.make_async_remote_copy(
            src_ref=src, dst_ref=dst, send_sem=send.at[i], recv_sem=recv.at[i],
            device_id=where, device_id_type=MESH,
        ).start()

    def dummy(ref, i):
        return pltpu.make_async_remote_copy(
            src_ref=ref, dst_ref=ref, send_sem=send.at[i], recv_sem=recv.at[i],
            device_id={"seq": sib, "dp": d}, device_id_type=MESH,
        )

    def arrived(ref, i):
        dummy(ref, i).wait_recv()

    def sent(ref, i):
        dummy(ref, i).wait_send()

    barrier = pltpu.get_barrier_semaphore()

    def greet(where):
        pl.semaphore_signal(barrier, inc=1, device_id=where, device_id_type=MESH)

    @pl.loop(1, SEQ)
    def _(k):
        greet({"seq": (s + k) % SEQ, "dp": d})

    for k in range(4):
        greet({"seq": ((zl + k) % 4) * 16 + y * 2 + core, "dp": (1 - zh) * 4 + x})
    for k in range(1, 4):
        greet(at_x(k))
        greet({"seq": sib, "dp": zh * 4 + (x + k) % 4})

    lane = lax.broadcasted_iota(jnp.int32, (1, HALF), 1)

    def pack_edges(read, dst):
        for side in range(2):
            total = None
            for k in range(8):
                rows = pl.ds(96 * k, 96)
                part = read(1 - side, rows).astype(F32)
                part = pltpu.roll(part, (16 * k + 16 * (1 - side)) % HALF, 1)
                keep = (lane >= 16 * k) & (lane < 16 * k + 16)
                total = jnp.where(keep, part, 0.0 if total is None else total)
            dst[side] = total.astype(BF)

    left_linked = link_ref[0, s] >= 0
    right_linked = link_ref[0, (s + 1) % SEQ] >= 0

    def halo_keep(width):
        return ((lane < width) & right_linked) | ((lane >= HALF - width) & left_linked)

    def unpack_edges(src, dst):
        from_left = src[0].astype(F32)
        from_right = src[1].astype(F32)
        for k in range(8):
            left = pltpu.roll(from_left, (HALF - 16 - 16 * k) % HALF, 1)
            right = pltpu.roll(from_right, (HALF - 16 * k) % HALF, 1)
            tile = jnp.where(lane < HALF // 2, right, left)
            dst[pl.ds(96 * k, 96), :] = jnp.where(halo_keep(16), tile, 0.0)

    pack_edges(lambda j, rows: x_ref[0, rows, pl.ds(HALF * j, HALF)], edge_s)

    for t in range(SEQ):
        block = cot_ref[0, :, pl.ds(HALF * t, HALF)]
        stage[t] = jnp.concatenate(
            [block.astype(F32), jnp.zeros((PAD - OWN, HALF), F32)], axis=0
        ).astype(BF)

    row = lax.broadcasted_iota(jnp.int32, (HALF, 112), 0)
    col = lax.broadcasted_iota(jnp.int32, (HALF, 112), 1)
    inner = row % PAD
    source = OWN * (2 * ((row // PAD) % 4) + row // 64) + inner
    pick = jnp.where((inner < OWN) & (source == col), 1.0, 0.0).astype(BF)
    own_rows = jnp.dot(pick, proj_ref[...], preferred_element_type=F32).astype(BF)
    pfull[0, d] = own_rows[:64]
    pfull[1, d] = own_rows[64:]

    pl.semaphore_wait(barrier, SEQ - 1 + 4 + 6)

    push(edge_s.at[0], edge_r.at[0], 0, {"seq": (s + 1) % SEQ, "dp": d})
    push(edge_s.at[1], edge_r.at[1], 1, {"seq": (s + SEQ - 1) % SEQ, "dp": d})
    partner = {"seq": s, "dp": (1 - zh) * 4 + x}
    push(pfull.at[core, d], pfull.at[core, d], 2, partner)
    for k in (1, 3, 2):
        push(pfull.at[core, d], pfull.at[core, d], 2 + k, at_x(k))
    me = core * 32 + zl * 8 + y
    @pl.loop(1, SEQ)
    def _(k):
        t = (s + k) % SEQ
        push(stage.at[t], cot.at[me], 6, {"seq": t, "dp": d})

    cot[me] = stage[s]

    six = jnp.concatenate([taps_ref[k] for k in range(3)] + [jnp.zeros((2, C), F32)], axis=0)
    wcol[...] = jnp.transpose(six)
    d0 = dil_ref[0]

    def weights(rows):
        return [[wcol[rows, 2 * k + b:2 * k + b + 1] for k in range(3)] for b in range(2)]

    arrived(edge_r.at[0], 0)
    arrived(edge_r.at[1], 1)
    unpack_edges(edge_r, halo)

    @pl.loop(0, C // SLAB)
    def _(i):
        rows = pl.ds(pl.multiple_of(i * SLAB, SLAB), SLAB)
        w = weights(rows)
        xs = [x_ref[0, rows, :HALF].astype(F32), x_ref[0, rows, HALF:].astype(F32), halo[rows, :]]
        acts = []
        for j in range(3):
            act, slope = gelu_pair(xs[j])
            acts.append(act)
            a0[j, rows, :] = act
            if j < 2:
                s0[j, rows, :] = slope
        lo, hi = earlier(acts, lane, d0), later(acts, lane, d0)
        ones = []
        acts1 = []
        for j in range(3):
            v = rounded(xs[j] + ((w[0][0] * lo[j] + w[0][1] * acts[j]) + w[0][2] * hi[j]))
            if j == 2:
                v = jnp.where(halo_keep(8), v, 0.0)
            ones.append(v)
            act, slope = gelu_pair(v)
            acts1.append(act)
            a1[j, rows, :] = act
            s1[j, rows, :] = slope
        lo, hi = earlier(acts1, lane, LAST_DILATION), later(acts1, lane, LAST_DILATION)
        for j in range(2):
            v = ones[j] + ((w[1][0] * lo[j] + w[1][1] * acts1[j]) + w[1][2] * hi[j])
            x2[rows, HALF * j:HALF * (j + 1)] = v.astype(BF)

    two = lax.broadcasted_iota(jnp.int32, (ROWS, HALF), 0) // 2
    pair = two == lax.broadcasted_iota(jnp.int32, (ROWS, HALF), 1)
    halves = jnp.where(pair, 0.5, 0.0).astype(BF)
    pooled[...] = jnp.dot(x2[...], halves, preferred_element_type=F32).astype(BF)
    push(pooled, pooled_sib, 7, {"seq": sib, "dp": d})

    other = (1 - zh) * 4 + x
    sibling = {"seq": sib, "dp": d}
    arrived(pfull.at[core, other], 2)
    for k in (1, 3, 2):
        push(pfull.at[core, other], pfull.at[core, other], 7 + k, at_x(k))
    push(pfull.at[core, other], pfull.at[core, other], 11, sibling)

    arrived(cot.at[pl.ds(0, SEQ - 1)], 6)
    push(cot.at[pl.ds((1 - core) * 32, 32)], cot_sib, 12, sibling)
    arrived(pooled_sib, 7)
    arrived(cot_sib, 12)
    mine = cot[pl.ds(core * 32, 32)].reshape(512, HALF)
    theirs = cot_sib[...].reshape(512, HALF)
    nt = (((1,), (1,)), ((), ()))
    for j in (2, 0, 1):
        cols = pl.ds(256 * j, 256)
        part = lax.dot_general(mine, pooled[cols, :], nt, preferred_element_type=F32)
        part = part + lax.dot_general(theirs, pooled_sib[cols, :], nt, preferred_element_type=F32)
        part = part.astype(BF)
        if j == 2:
            b_s1[...] = part.reshape(4, 8, PAD, 256)
            @pl.loop(1, 8)
            def _(k):
                yy = (y + k) % 8
                push(b_s1.at[:, yy], b_r1.at[y], 13, at_y(yy))
        else:
            a_s1[2 * j] = part[:, :HALF].reshape(4, 8, PAD, HALF)
            a_s1[2 * j + 1] = part[:, HALF:].reshape(4, 8, PAD, HALF)
    for k in (1, 3, 2):
        push(a_s1.at[(x + k) % 4], a_r1.at[x], 14, at_x(k))
    b_r1[y] = b_s1[:, y]
    a_r1[x] = a_s1[x]

    for k in (1, 3, 2):
        arrived(pfull.at[core, d], 2 + k)
        blk = zh * 4 + (x + 4 - k) % 4
        push(pfull.at[core, blk], pfull.at[core, blk], 14 + k, sibling)
    for k in (1, 3, 2):
        arrived(pfull.at[core, d], 7 + k)
        blk = (1 - zh) * 4 + (x + 4 - k) % 4
        push(pfull.at[core, blk], pfull.at[core, blk], 17 + k, sibling)
    arrived(pfull.at[core, d], 11)
    for k in (1, 2, 3):
        arrived(pfull.at[core, d], 14 + k)
        arrived(pfull.at[core, d], 17 + k)
    back = lax.dot_general(
        cot[...].reshape(SEQ * PAD, HALF), pfull[...].reshape(SEQ * PAD, C),
        (((0,), (0,)), ((), ())), preferred_element_type=F32,
    )
    back = (0.5 * back).astype(BF)
    two = lax.broadcasted_iota(jnp.int32, (HALF, ROWS), 1) // 2
    spread = jnp.where(two == lax.broadcasted_iota(jnp.int32, (HALF, ROWS), 0), 1.0, 0.0).astype(BF)
    g2[...] = lax.dot_general(back, spread, (((0,), (0,)), ((), ())), preferred_element_type=F32)
    pack_edges(lambda j, rows: g2[rows, HALF * j:HALF * (j + 1)], gedge_s)
    push(gedge_s.at[0], gedge_r.at[0], 21, {"seq": (s + 1) % SEQ, "dp": d})
    push(gedge_s.at[1], gedge_r.at[1], 22, {"seq": (s + SEQ - 1) % SEQ, "dp": d})
    arrived(gedge_r.at[0], 21)
    arrived(gedge_r.at[1], 22)
    unpack_edges(gedge_r, halo)

    @pl.loop(0, C // SLAB)
    def _(i):
        rows = pl.ds(pl.multiple_of(i * SLAB, SLAB), SLAB)
        w = weights(rows)
        cols = jnp.zeros((SLAB, HALF), F32)

        def tap_columns(cols, g, a, dist, b):
            shifted = (earlier(a, lane, dist), a, later(a, lane, dist))
            for k in range(3):
                total = jnp.sum(g[0] * shifted[k][0] + g[1] * shifted[k][1], axis=1, keepdims=True)
                cols = jnp.where(lane == 2 * k + b, total, cols)
            return cols

        g = [g2[rows, :HALF], g2[rows, HALF:], halo[rows, :]]
        cols = tap_columns(cols, g, [a1[j, rows, :] for j in range(3)], LAST_DILATION, 1)
        lo, hi = earlier(g, lane, LAST_DILATION), later(g, lane, LAST_DILATION)
        g1 = []
        for j in range(3):
            conv = (w[1][0] * hi[j] + w[1][1] * g[j]) + w[1][2] * lo[j]
            g1.append(rounded(g[j] + conv * s1[j, rows, :]))
        g1[2] = jnp.where(halo_keep(8), g1[2], 0.0)
        cols = tap_columns(cols, g1, [a0[j, rows, :] for j in range(3)], d0, 0)
        lo, hi = earlier(g1, lane, d0), later(g1, lane, d0)
        for j in range(2):
            conv = (w[0][0] * hi[j] + w[0][1] * g1[j]) + w[0][2] * lo[j]
            out_ref[0, rows, HALF * j:HALF * (j + 1)] = (g1[j] + conv * s0[j, rows, :]).astype(BF)
        tcol[rows, :] = cols

    flat = jnp.transpose(tcol[...])[:8]
    t_s[0] = flat[:, :384]
    t_s[1] = flat[:, 384:]
    slot = x * 2 + core
    t_r1[slot] = t_s[core]
    for k in range(4):
        for c in range(2):
            cc = (core + c) % 2
            if k or c:
                push(t_s.at[cc], t_r1.at[slot], 23, at_x_core((x + k) % 4, cc))

    def total(ref):
        parts = [ref[i].astype(F32) for i in range(ref.shape[0])]
        while len(parts) > 1:
            parts = [a + b for a, b in zip(parts[::2], parts[1::2])]
        return parts[0]

    arrived(b_r1.at[pl.ds(0, 7)], 13)
    b_s2[...] = total(b_r1).astype(BF)
    @pl.loop(1, 8)
    def _(k):
        zz = (z8 + k) % 8
        push(b_s2.at[zz % 4], b_r2.at[z8], 24, at_z(zz))
    b_r2[z8] = b_s2[zl]

    arrived(a_r1.at[pl.ds(0, 3)], 14)
    a_s2[...] = total(a_r1).astype(BF)
    @pl.loop(1, 8)
    def _(k):
        yy = (y + k) % 8
        push(a_s2.at[:, yy], a_r2.at[y], 25, at_y(yy))
    a_r2[y] = a_s2[:, y]

    arrived(t_r1.at[pl.ds(0, 7)], 23)
    t_r2[y] = total(t_r1)
    @pl.loop(1, 8)
    def _(k):
        push(t_r2.at[y], t_r2.at[y], 26, at_y((y + k) % 8))

    arrived(b_r2.at[pl.ds(0, 7)], 24)
    b_r3[x] = total(b_r2)
    for k in (1, 3, 2):
        push(b_r3.at[x], b_r3.at[x], 27, at_x(k))

    arrived(a_r2.at[pl.ds(0, 7)], 25)
    a_s3[...] = total(a_r2).astype(BF)
    @pl.loop(1, 8)
    def _(k):
        zz = (z8 + k) % 8
        push(a_s3.at[zz % 4], a_r3.at[z8], 28, at_z(zz))
    a_r3[z8] = a_s3[zl]

    arrived(t_r2.at[pl.ds(0, 7)], 26)
    t_r3[z8] = total(t_r2)
    @pl.loop(1, 8)
    def _(k):
        push(t_r3.at[z8], t_r3.at[z8], 29, at_z((z8 + k) % 8))

    arrived(a_r3.at[pl.ds(0, 7)], 28)
    a_r4[x] = total(a_r3)
    for k in (1, 3, 2):
        push(a_r4.at[x], a_r4.at[x], 30, at_x(k))

    arrived(t_r3.at[pl.ds(0, 7)], 29)
    t_f[core] = total(t_r3)
    push(t_f.at[core], t_f.at[core], 31, sibling)

    scale = 1.0 / math.sqrt(SEQ * DP * HALF)
    arrived(b_r3.at[pl.ds(0, 3)], 27)
    pg_ref[:, 512:] = total(b_r3)[:OWN] * scale
    arrived(a_r4.at[pl.ds(0, 3)], 30)
    for j in range(4):
        pg_ref[:, HALF * j:HALF * (j + 1)] = a_r4[j][:OWN] * scale
    arrived(t_f.at[core], 31)
    for h in range(2):
        for k in range(3):
            tg_ref[k, :, 384 * h:384 * (h + 1)] = t_f[h][2 * k:2 * k + 2] * scale

    sent(edge_s.at[0], 0)
    sent(edge_s.at[1], 1)
    for i in range(2, 6):
        sent(pfull.at[0, 0], i)
    sent(stage.at[pl.ds(0, SEQ - 1)], 6)
    sent(pooled, 7)
    for i in (8, 9, 10, 11, 15, 16, 17, 18, 19, 20):
        sent(pfull.at[0, 0], i)
    sent(cot_sib, 12)
    sent(b_r1.at[pl.ds(0, 7)], 13)
    sent(a_r1.at[pl.ds(0, 3)], 14)
    sent(gedge_s.at[0], 21)
    sent(gedge_s.at[1], 22)
    sent(t_r1.at[pl.ds(0, 7)], 23)
    sent(b_r2.at[pl.ds(0, 7)], 24)
    sent(a_r2.at[pl.ds(0, 7)], 25)
    sent(t_r2.at[pl.ds(0, 7)], 26)
    sent(b_r3.at[pl.ds(0, 3)], 27)
    sent(a_r3.at[pl.ds(0, 7)], 28)
    sent(t_r3.at[pl.ds(0, 7)], 29)
    sent(a_r4.at[pl.ds(0, 3)], 30)
    sent(t_f.at[0], 31)


SCRATCH = [
    ((SEQ, PAD, HALF), BF),
    ((SEQ, PAD, HALF), BF),
    ((32, PAD, HALF), BF),
    ((2, DP, 64, C), BF),
    ((2, 96, HALF), BF),
    ((2, 96, HALF), BF),
    ((2, 96, HALF), BF),
    ((2, 96, HALF), BF),
    ((C, HALF), F32),
    ((C, 8), F32),
    ((3, C, HALF), F32),
    ((3, C, HALF), F32),
    ((2, C, HALF), F32),
    ((3, C, HALF), F32),
    ((C, ROWS), BF),
    ((C, HALF), BF),
    ((C, HALF), BF),
    ((C, ROWS), F32),
    ((C, HALF), F32),
    ((4, 4, 8, PAD, HALF), BF),
    ((4, 4, 8, PAD, HALF), BF),
    ((4, 8, PAD, HALF), BF),
    ((8, 4, PAD, HALF), BF),
    ((4, PAD, HALF), BF),
    ((8, PAD, HALF), BF),
    ((4, PAD, HALF), F32),
    ((4, 8, PAD, 256), BF),
    ((8, 4, PAD, 256), BF),
    ((4, PAD, 256), BF),
    ((8, PAD, 256), BF),
    ((4, PAD, 256), F32),
    ((2, 8, 384), F32),
    ((8, 8, 384), F32),
    ((8, 8, 384), F32),
    ((8, 8, 384), F32),
    ((2, 8, 384), F32),
]


def local(sequence_acts, taps, dilations, left_link, projection, head_cotangent):
    vmem = pl.BlockSpec(memory_space=pltpu.VMEM)
    smem = pl.BlockSpec(memory_space=pltpu.SMEM)
    grad, weight, tap_grads = pl.pallas_call(
        kernel,
        out_shape=(
            jax.ShapeDtypeStruct((1, C, ROWS), BF),
            jax.ShapeDtypeStruct((OWN, C), F32),
            jax.ShapeDtypeStruct((3, 2, C), F32),
        ),
        in_specs=[vmem, vmem, smem, smem, vmem, vmem],
        out_specs=(vmem, vmem, vmem),
        scratch_shapes=[pltpu.VMEM(shape, kind) for shape, kind in SCRATCH]
        + [pltpu.SemaphoreType.DMA((32,)), pltpu.SemaphoreType.DMA((32,))],
        compiler_params=pltpu.CompilerParams(
            collective_id=0, has_side_effects=True, vmem_limit_bytes=48 * 1024 * 1024
        ),
        cost_estimate=pl.CostEstimate(
            flops=1_000_000_000, bytes_accessed=4_000_000, transcendentals=600_000
        ),
    )(sequence_acts, jnp.transpose(taps, (2, 0, 1)), dilations, left_link, projection, head_cotangent)
    return grad, weight, jnp.transpose(tap_grads, (1, 2, 0))


def solution(mesh):
    placed = (P("dp", None, "seq"), P(), P(), P("dp", None), P("dp", None), P("dp", "seq", None))
    return jax.shard_map(
        local,
        mesh=mesh,
        in_specs=placed,
        out_specs=(P("dp", None, "seq"), P("seq", None), P()),
        check_vma=False,
    )
```

time: 457 us -> 72.5 us (0.16)
  waiting for transfers between devices: 171 us -> 0 us
  blocking collectives: 105 us -> 0 us
  Pallas kernels: 0 us -> 65.3 us
  other arithmetic: 54.7 us -> 0 us
  starting transfers between devices: 50.8 us -> 0 us
  local copies, waits for them, and re-layouts: 50.2 us -> 6.21 us
  between operations: 19.7 us -> 0.66 us
    psum x1 -> x0, waiting for transfers between devices: 168 us -> none  [local(): lax.psum((local_weight, local_taps), ('seq', 'dp'))]
    psum x1 -> x0, blocking collectives: 105 us -> none  [local(): lax.psum((local_weight, local_taps), ('seq', 'dp'))]
    pallas_call x0 -> x1, Pallas kernels: none -> 65.3 us  [local(): pl.pallas_call(kernel, out_shape=(jax.ShapeDtypeStruct((1, C, ROWS), BF),...]
    unnamed x1 -> x0, other arithmetic: 45.2 us -> none
    ppermute x8 -> x0, starting transfers between devices: 36 us -> none  [the longest x4 25 us: with_halo(): after = lax.ppermute(leading, axis, down)]
    slice x10 -> x0, local copies, waits for them, and re-layouts: 17.6 us -> none  [the longest x1 8.21 us: local(): running_state[:, 0::2].astype(jnp.float32)]
    unnamed x16 -> x15, local copies, waits for them, and re-layouts: 22.9 us -> 6.21 us
    all_to_all x1 -> x0, starting transfers between devices: 14.7 us -> none  [local(): lax.all_to_all(head_cotangent, 'seq', split_axis=2, concat_axis=1, tiled=...]
  transfers between devices with their start and end apart: 11 -> 0, of which waited for: 3 -> 0; matrix products, arithmetic and copies ran while one was open for 18% -> 0% of each run, Pallas kernels for 0% -> 0%
where the time goes in v1:
time: 72.5 us; the launch traced here: 72.2 us
  Pallas kernels  65.3 us (90%)
  local copies, waits for them, and re-layouts  6.21 us (9%)
    pallas_call x1, Pallas kernels, local(): pl.pallas_call(kernel, out_shape=(jax.ShapeDtypeStruct((1, C, ROWS), BF),...  65.3 us
    unnamed x15, local copies, waits for them, and re-layouts  6.21 us

profile of v1, /device:TPU:1, one launch (start us, length us, event | category | flops | bytes accessed | tf_op | source)
XLA Modules:
  0.0 72.2 jit_solution(1428823165751744684)
XLA Ops:
  0.6 0.0 copy-start.5
  0.6 0.0 copy-start.4
  0.7 0.6 copy-done.5
  1.3 0.0 copy-done.4
  1.3 0.0 copy-start
  1.3 1.0 %copy-done = bf16[1,768,256]{2,1,0:T(8,128)(2,1)S(1)} copy-done((bf16[1,768,256]{2,1,0:T(8,128)(2,1)S(1)}, bf16[1,768,256]{2,1,0:T(8,128)(2,1)}, u32[]{:S(2)}) %copy-start) | copy-done | bytes 393240
  2.3 0.0 copy-start.1
  2.3 0.9 %copy-done.1 = bf16[1,14,8192]{2,1,0:T(8,128)(2,1)S(1)} copy-done((bf16[1,14,8192]{2,1,0:T(8,128)(2,1)S(1)}, bf16[1,14,8192]{2,1,0:T(8,128)(2,1)}, u32[]{:S(2)}) %copy-start.1) | copy-done | bytes 229400
  3.3 0.0 copy-start.2
  3.3 0.9 %copy-done.2 = bf16[112,768]{1,0:T(8,128)(2,1)S(1)} copy-done((bf16[112,768]{1,0:T(8,128)(2,1)S(1)}, bf16[112,768]{1,0:T(8,128)(2,1)}, u32[]{:S(2)}) %copy-start.2) | copy-done | bytes 172056
  4.2 0.0 copy-start.3
  4.2 0.7 copy-done.3
  4.9 65.3 %shard_map.85 = (bf16[1,768,256]{2,1,0:T(8,128)(2,1)S(1)}, f32[14,768]{1,0:T(8,128)S(1)}, f32[3,2,768]{2,1,0:T(2,128)S(1)}) custom-call(bf16[1,768,256]{2,1,0:T(8,128)(2,1)S(1)} %copy-done, f32[3,2,768]{2,1,0:T(2,128)S(1)} %bitcast.3, s32[2]{0:T(128)S(1)} %copy-done.4, s32[1,64]{1,0:T(1,128)S(1)} %copy-done.5, bf16[112,768]{1,0:T(8,128)(2,1)S(1)} %copy-done.2, ...), custom_call_target="tpu_custom_call" | custom-call | flops 1000000000 | bytes 4000000 | tf_op jit(solution)/shard_map/pallas_call | solution.py:453
  70.2 0.7 %copy.12 = bf16[1,768,256]{2,1,0:T(8,128)(2,1)} copy(bf16[1,768,256]{2,1,0:T(8,128)(2,1)S(1)} %get-tuple-element.12) | data formatting | bytes 786432
  71.0 0.6 copy.13
  71.6 0.6 copy.14
Async XLA Ops:
  0.6 0.7 copy-start.5
  0.6 0.7 copy-start.4
  1.3 1.0 %copy-start = (bf16[1,768,256]{2,1,0:T(8,128)(2,1)S(1)}, bf16[1,768,256]{2,1,0:T(8,128)(2,1)}, u32[]{:S(2)}) copy-start(bf16[1,768,256]{2,1,0:T(8,128)(2,1)} %x_ref.1) | copy-start | bytes 1179652
  2.3 0.9 %copy-start.1 = (bf16[1,14,8192]{2,1,0:T(8,128)(2,1)S(1)}, bf16[1,14,8192]{2,1,0:T(8,128)(2,1)}, u32[]{:S(2)}) copy-start(bf16[1,14,8192]{2,1,0:T(8,128)(2,1)} %cot_ref.1) | copy-start | bytes 688132
  3.3 0.9 %copy-start.2 = (bf16[112,768]{1,0:T(8,128)(2,1)S(1)}, bf16[112,768]{1,0:T(8,128)(2,1)}, u32[]{:S(2)}) copy-start(bf16[112,768]{1,0:T(8,128)(2,1)} %proj_ref.1) | copy-start | bytes 516100
  4.2 0.7 %copy-start.3 = (f32[2,768,3]{1,0,2:T(2,128)S(1)}, f32[2,768,3]{1,0,2:T(2,128)}, u32[]{:S(2)}) copy-start(f32[2,768,3]{1,0,2:T(2,128)} %param.7) | copy-start | bytes 55300

commit v2 on v1

v2 whole, which is shorter than its diff:
```python
import functools
import math

import jax
import jax.numpy as jnp
from jax import lax
from jax.experimental import pallas as pl
from jax.experimental.pallas import tpu as pltpu
from jax.sharding import PartitionSpec as P

MESH = pl.DeviceIdType.MESH
BF = jnp.bfloat16
F32 = jnp.float32

C = 768
ROWS = 256
HALF = 128
SEQ = 64
DP = 8
OWN = 14
PAD = 16
SLAB = 64
LAST_DILATION = 8
Z_PART, X_PART, SIB_PART = 32, 36, 40
FAR_FIRST = sorted(
    range(1, SEQ),
    key=lambda m: -((0, 1, 2, 2)[m >> 4] + (0, 1, 2, 2, 4, 3, 2, 2)[(m >> 1) & 7]),
)
GELU = 0.7978845608028654


def gelu_pair(v):
    th = jnp.tanh(GELU * (v + 0.044715 * v * v * v))
    act = 0.5 * v * (1.0 + th)
    slope = 0.5 * (1.0 + th) + 0.5 * v * (1.0 - th * th) * GELU * (1.0 + 3.0 * 0.044715 * v * v)
    return act, slope


def rounded(v):
    return v.astype(BF).astype(F32)


def earlier(tiles, lane, d):
    turned = [pltpu.roll(t, d, 1) for t in tiles]
    return [jnp.where(lane < d, turned[j - 1], turned[j]) for j in range(len(tiles))]


def later(tiles, lane, d):
    turned = [pltpu.roll(t, HALF - d, 1) for t in tiles]
    n = len(tiles)
    return [jnp.where(lane >= HALF - d, turned[(j + 1) % n], turned[j]) for j in range(n)]


def kernel(
    x_in, taps_in, dil_in, link_in, proj_in, cot_in,
    out_ref, pg_ref, tg_ref,
    x_ref, taps_ref, proj_ref, cot_ref, dil_ref, link_ref,
    stage, cot, cot_sib, pfull, edge_s, edge_r, cot_t, halo, wide,
    a0, a1, s0, s1, x2, pooled, pooled_sib, g2, g1, moved, prods,
    a_s1, a_r1, a_s2, a_r2, a_s3, a_r3, a_r4, b_s1, b_r1, b_s2, b_r2, b_r3,
    t_s, t_r1, t_r2, t_r3, t_f,
    send, recv, load,
):
    s = lax.axis_index("seq")
    d = lax.axis_index("dp")
    core = s % 2
    y = (s // 2) % 8
    zl = s // 16
    x = d % 4
    zh = d // 4
    z8 = zh * 4 + zl
    sib = s + 1 - 2 * core

    def at_x(k):
        return {"seq": s, "dp": zh * 4 + (x + k) % 4}

    def at_x_core(xx, cc):
        return {"seq": s - core + cc, "dp": zh * 4 + xx}

    def at_y(yy):
        return {"seq": zl * 16 + yy * 2 + core, "dp": d}

    def at_z(zz):
        return {"seq": (zz % 4) * 16 + y * 2 + core, "dp": (zz // 4) * 4 + x}

    whole = {
        0: edge_s.at[0], 1: edge_s.at[0], 6: stage.at[pl.ds(0, SEQ - 1)], 7: pooled, 12: cot_sib,
        13: b_r1.at[pl.ds(0, 7)], 14: a_r1.at[pl.ds(0, 3)], 21: cot_t.at[pl.ds(0, PAD)], 22: cot_t.at[pl.ds(0, PAD)],
        23: t_r1.at[pl.ds(0, 7)], 24: b_r2.at[pl.ds(0, 7)], 25: a_r2.at[pl.ds(0, 7)],
        26: t_r2.at[pl.ds(0, 7)], 27: b_r3.at[pl.ds(0, 3)], 28: a_r3.at[pl.ds(0, 7)],
        29: t_r3.at[pl.ds(0, 7)], 30: a_r4.at[pl.ds(0, 3)], 31: t_f.at[0],
        3: pfull.at[0, pl.ds(0, 3)], 4: pfull.at[0, pl.ds(0, 4)],
    }
    for i in range(4):
        whole[Z_PART + i] = pfull.at[0, 0, pl.ds(0, PAD)]
        whole[X_PART + i] = pfull.at[0, pl.ds(0, 3), pl.ds(0, PAD)]
        whole[SIB_PART + i] = pfull.at[0, pl.ds(0, 4), pl.ds(0, PAD)]
    started, ended = [], []
    sibling = {"seq": sib, "dp": d}

    def push(src, dst, i, where):
        if i not in started:
            started.append(i)
        pltpu.make_async_remote_copy(
            src_ref=src, dst_ref=dst, send_sem=send.at[i], recv_sem=recv.at[i],
            device_id=where, device_id_type=MESH,
        ).start()

    def dummy(i):
        ref = whole[i]
        return pltpu.make_async_remote_copy(
            src_ref=ref, dst_ref=ref, send_sem=send.at[i], recv_sem=recv.at[i],
            device_id={"seq": sib, "dp": d}, device_id_type=MESH,
        )

    def arrived(i):
        ended.append(i)
        dummy(i).wait_recv()

    def finish():
        for i in started:
            if i not in ended:
                arrived(i)
            if i in range(Z_PART, Z_PART + 4):
                @pl.when((zl == 0) | (zl == 3))
                def _():
                    dummy(i).wait_send()
                    dummy(i).wait_send()
            else:
                dummy(i).wait_send()

    loads = [
        pltpu.make_async_copy(a, b, load.at[i])
        for i, (a, b) in enumerate(
            (
                (cot_in, cot_ref), (x_in, x_ref), (proj_in, proj_ref), (taps_in, taps_ref),
                (dil_in, dil_ref), (link_in, link_ref),
            )
        )
    ]
    for copy in loads:
        copy.start()

    barrier = pltpu.get_barrier_semaphore()

    def greet(where):
        pl.semaphore_signal(barrier, inc=1, device_id=where, device_id_type=MESH)

    @pl.loop(1, SEQ)
    def _(k):
        greet({"seq": (s + k) % SEQ, "dp": d})

    for k in range(4):
        greet({"seq": ((zl + k) % 4) * 16 + y * 2 + core, "dp": (1 - zh) * 4 + x})
    for k in range(1, 4):
        greet(at_x(k))
        greet({"seq": sib, "dp": zh * 4 + (x + k) % 4})

    lane = lax.broadcasted_iota(jnp.int32, (1, HALF), 1)

    def pack_edges(read, dst):
        for side in range(2):
            total = None
            for k in range(8):
                rows = pl.ds(96 * k, 96)
                part = read(1 - side, rows).astype(F32)
                part = pltpu.roll(part, (16 * k + 16 * (1 - side)) % HALF, 1)
                keep = (lane >= 16 * k) & (lane < 16 * k + 16)
                total = jnp.where(keep, part, 0.0 if total is None else total)
            dst[side] = total.astype(BF)

    def halo_keep(width):
        return ((lane < width) & right_linked) | ((lane >= HALF - width) & left_linked)

    def unpack_edges(src, dst):
        from_left = src[0].astype(F32)
        from_right = src[1].astype(F32)
        for k in range(8):
            left = pltpu.roll(from_left, (HALF - 16 - 16 * k) % HALF, 1)
            right = pltpu.roll(from_right, (HALF - 16 * k) % HALF, 1)
            tile = jnp.where(lane < HALF // 2, right, left)
            dst[pl.ds(96 * k, 96), :] = jnp.where(halo_keep(16), tile, 0.0)

    loads[0].wait()
    for t in range(SEQ):
        block = cot_ref[0, :, pl.ds(HALF * t, HALF)]
        stage[t] = jnp.concatenate(
            [block.astype(F32), jnp.zeros((PAD - OWN, HALF), F32)], axis=0
        ).astype(BF)

    loads[1].wait()
    pack_edges(lambda j, rows: x_ref[0, rows, pl.ds(HALF * j, HALF)], edge_s)

    loads[2].wait()
    row = lax.broadcasted_iota(jnp.int32, (64, 112), 0)
    col = lax.broadcasted_iota(jnp.int32, (64, 112), 1)
    inner = row % PAD
    source = OWN * (2 * (row // PAD) + core) + inner
    pick = jnp.where((inner < OWN) & (source == col), 1.0, 0.0).astype(BF)
    pfull[core, d] = jnp.dot(pick, proj_ref[...], preferred_element_type=F32).astype(BF)

    pl.semaphore_wait(barrier, SEQ - 1 + 4 + 6)

    push(edge_s.at[0], edge_r.at[0], 0, {"seq": (s + 1) % SEQ, "dp": d})
    push(edge_s.at[1], edge_r.at[1], 1, {"seq": (s + SEQ - 1) % SEQ, "dp": d})
    for edge, step in ((0, -1), (3, 1)):
        @pl.when(zl == edge)
        def _():
            for i in range(4):
                rows = pfull.at[core, d, pl.ds(PAD * i, PAD)]
                for far in (2, 1):
                    push(rows, rows, Z_PART + i, at_z((z8 + 8 + far * step) % 8))
    for k in (2, 1, 3):
        push(pfull.at[core, d], pfull.at[core, d], 3, at_x(k))
    other = (1 - zh) * 4

    def pass_x(i):
        arrived(Z_PART + i)
        rows = pfull.at[core, other + x, pl.ds(PAD * i, PAD)]
        for k in (2, 1, 3):
            push(rows, rows, X_PART + i, at_x(k))

    def pass_core(i):
        arrived(X_PART + i)
        rows = pfull.at[core, pl.ds(other, 4), pl.ds(PAD * i, PAD)]
        push(rows, rows, SIB_PART + i, sibling)

    me = core * 32 + zl * 8 + y
    for m in FAR_FIRST:
        t = s ^ m
        push(stage.at[t], cot.at[me], 6, {"seq": t, "dp": d})

    cot[me] = stage[s]

    for copy in loads[3:]:
        copy.wait()
    left_linked = link_ref[0, s] >= 0
    right_linked = link_ref[0, (s + 1) % SEQ] >= 0
    six = jnp.concatenate([taps_ref[k] for k in range(3)] + [jnp.zeros((2, C), F32)], axis=0)
    six = jnp.transpose(six)
    for i in range(6):
        wide[i] = jnp.broadcast_to(six[:, i:i + 1], (C, HALF))
    d0 = dil_ref[0]

    def weights(rows):
        return [[wide[2 * k + b, rows, :] for k in range(3)] for b in range(2)]

    @pl.loop(0, C // SLAB)
    def _(i):
        rows = pl.ds(pl.multiple_of(i * SLAB, SLAB), SLAB)
        for j in range(2):
            act, slope = gelu_pair(x_ref[0, rows, HALF * j:HALF * (j + 1)].astype(F32))
            a0[j, rows, :] = act
            s0[j, rows, :] = slope

    arrived(0)
    arrived(1)
    unpack_edges(edge_r, halo)

    def forward(first, last):
        @pl.loop(first, last)
        def _(i):
            rows = pl.ds(pl.multiple_of(i * SLAB, SLAB), SLAB)
            w = weights(rows)
            xs = [x_ref[0, rows, :HALF].astype(F32), x_ref[0, rows, HALF:].astype(F32), halo[rows, :]]
            acts = [a0[0, rows, :], a0[1, rows, :], gelu_pair(xs[2])[0]]
            lo, hi = earlier(acts, lane, d0), later(acts, lane, d0)
            ones = []
            acts1 = []
            for j in range(3):
                v = rounded(xs[j] + ((w[0][0] * lo[j] + w[0][1] * acts[j]) + w[0][2] * hi[j]))
                if j == 2:
                    v = jnp.where(halo_keep(8), v, 0.0)
                ones.append(v)
                act, slope = gelu_pair(v)
                acts1.append(act)
                if j < 2:
                    a1[j, rows, :] = act
                s1[j, rows, :] = slope
            lo, hi = earlier(acts1, lane, LAST_DILATION), later(acts1, lane, LAST_DILATION)
            for j in range(2):
                v = ones[j] + ((w[1][0] * lo[j] + w[1][1] * acts1[j]) + w[1][2] * hi[j])
                x2[rows, HALF * j:HALF * (j + 1)] = v.astype(BF)

    forward(0, 4)
    pass_x(0)
    forward(4, 8)
    pass_x(1)
    pass_x(2)
    forward(8, 12)
    pass_x(3)
    arrived(3)
    rows = pfull.at[core, pl.ds(zh * 4, 4)]
    push(rows, rows, 4, sibling)

    two = lax.broadcasted_iota(jnp.int32, (ROWS, HALF), 0) // 2
    pair = two == lax.broadcasted_iota(jnp.int32, (ROWS, HALF), 1)
    halves = jnp.where(pair, 0.5, 0.0).astype(BF)
    pooled[...] = jnp.dot(x2[...], halves, preferred_element_type=F32).astype(BF)
    push(pooled, pooled_sib, 7, {"seq": sib, "dp": d})

    arrived(6)
    push(cot.at[pl.ds((1 - core) * 32, 32)], cot_sib, 12, sibling)
    eye = lax.broadcasted_iota(jnp.int32, (HALF, HALF), 0) == lax.broadcasted_iota(jnp.int32, (HALF, HALF), 1)
    nt = (((1,), (1,)), ((), ()))
    cot_t[:HALF] = lax.dot_general(
        jnp.where(eye, 1.0, 0.0).astype(BF), cot[...].reshape(SEQ * PAD, HALF), nt,
        preferred_element_type=F32,
    ).astype(BF)
    push(cot_t.at[pl.ds(HALF - PAD, PAD)], cot_t.at[pl.ds(HALF + PAD, PAD)], 21, {"seq": (s + 1) % SEQ, "dp": d})
    push(cot_t.at[pl.ds(0, PAD)], cot_t.at[pl.ds(HALF, PAD)], 22, {"seq": (s + SEQ - 1) % SEQ, "dp": d})
    pass_core(0)
    pass_core(1)
    arrived(7)
    arrived(12)
    mine = cot[pl.ds(core * 32, 32)].reshape(512, HALF)
    theirs = cot_sib[...].reshape(512, HALF)
    for j in (2, 0, 1):
        cols = pl.ds(256 * j, 256)
        part = lax.dot_general(mine, pooled[cols, :], nt, preferred_element_type=F32)
        part = part + lax.dot_general(theirs, pooled_sib[cols, :], nt, preferred_element_type=F32)
        part = part.astype(BF)
        if j == 2:
            b_s1[...] = part.reshape(4, 8, PAD, 256)
            @pl.loop(1, 8)
            def _(k):
                yy = (y + k) % 8
                push(b_s1.at[:, yy], b_r1.at[y], 13, at_y(yy))
        else:
            a_s1[2 * j] = part[:, :HALF].reshape(4, 8, PAD, HALF)
            a_s1[2 * j + 1] = part[:, HALF:].reshape(4, 8, PAD, HALF)
    for k in (1, 3, 2):
        push(a_s1.at[(x + k) % 4], a_r1.at[x], 14, at_x(k))
    b_r1[y] = b_s1[:, y]
    a_r1[x] = a_s1[x]

    pass_core(2)
    pass_core(3)
    for i in (4, SIB_PART, SIB_PART + 1, SIB_PART + 2, SIB_PART + 3, 21, 22):
        arrived(i)
    back = jnp.dot(cot_t[...], pfull[...].reshape(SEQ * PAD, C), preferred_element_type=F32)
    back = (0.5 * back).astype(BF)
    ring = 3 * HALF
    shape = (HALF + 2 * PAD, ring)
    at = lax.broadcasted_iota(jnp.int32, shape, 0)
    to = lax.broadcasted_iota(jnp.int32, shape, 1)
    right = (to >= ROWS) & (to < ROWS + 16) & right_linked
    left = (to >= ring - 16) & left_linked
    origin = jnp.where(
        to < ROWS, to // 2,
        jnp.where(right, HALF + (to - ROWS) // 2, jnp.where(left, HALF + 24 + (to - ring + 16) // 2, -1)),
    )
    spread = jnp.where(at == origin, 1.0, 0.0).astype(BF)
    g2[...] = lax.dot_general(
        back, spread, (((0,), (0,)), ((), ())), preferred_element_type=F32
    ).astype(BF)

    def shifts(dist, length):
        at = lax.broadcasted_iota(jnp.int32, (ring, 2 * length), 0)
        to = lax.broadcasted_iota(jnp.int32, (ring, 2 * length), 1)
        low = to < length
        to = jnp.where(low, to - dist + ring, to - length + dist)
        to = jnp.where(to >= ring, to - ring, to)
        return jnp.where(at == to, 1.0, 0.0).astype(BF)

    def keep_product(rows, column, total):
        high = total.astype(BF)
        prods[rows, HALF * column:HALF * (column + 1)] = high
        low = (total - high.astype(F32)).astype(BF)
        prods[rows, HALF * (column + 6):HALF * (column + 7)] = low

    matrix1 = shifts(LAST_DILATION, ring)
    matrix0 = shifts(d0, ROWS)
    moved[...] = jnp.dot(g2[...], matrix1, preferred_element_type=F32)

    @pl.loop(0, C // SLAB)
    def _(i):
        rows = pl.ds(pl.multiple_of(i * SLAB, SLAB), SLAB)
        w = weights(rows)[1]
        g = [g2[rows, HALF * j:HALF * (j + 1)].astype(F32) for j in range(3)]
        lo = [moved[rows, HALF * j:HALF * (j + 1)] for j in range(3)]
        hi = [moved[rows, ring + HALF * j:ring + HALF * (j + 1)] for j in range(3)]
        for j in range(3):
            conv = (w[0] * hi[j] + w[1] * g[j]) + w[2] * lo[j]
            v = g[j] + conv * s1[j, rows, :]
            if j == 2:
                v = jnp.where(halo_keep(8), v, 0.0)
            g1[rows, HALF * j:HALF * (j + 1)] = v.astype(BF)
        for k, part in enumerate((hi, g, lo)):
            keep_product(rows, 2 * k + 1, a1[0, rows, :] * part[0] + a1[1, rows, :] * part[1])

    moved[:, :2 * ROWS] = jnp.dot(g1[...], matrix0, preferred_element_type=F32)

    @pl.loop(0, C // SLAB)
    def _(i):
        rows = pl.ds(pl.multiple_of(i * SLAB, SLAB), SLAB)
        w = weights(rows)[0]
        g = [g1[rows, HALF * j:HALF * (j + 1)].astype(F32) for j in range(2)]
        lo = [moved[rows, HALF * j:HALF * (j + 1)] for j in range(2)]
        hi = [moved[rows, ROWS + HALF * j:ROWS + HALF * (j + 1)] for j in range(2)]
        for j in range(2):
            conv = (w[0] * hi[j] + w[1] * g[j]) + w[2] * lo[j]
            out_ref[0, rows, HALF * j:HALF * (j + 1)] = (g[j] + conv * s0[j, rows, :]).astype(BF)
        for k, part in enumerate((hi, g, lo)):
            keep_product(rows, 2 * k, a0[0, rows, :] * part[0] + a0[1, rows, :] * part[1])

    which = lax.broadcasted_iota(jnp.int32, (8, 12 * HALF), 1) // HALF
    row = lax.broadcasted_iota(jnp.int32, (8, 12 * HALF), 0)
    ones = jnp.where(which % 6 == row, 1.0, 0.0).astype(BF)
    flat = lax.dot_general(ones, prods[...], nt, preferred_element_type=F32)
    t_s[0] = flat[:, :384]
    t_s[1] = flat[:, 384:]
    slot = x * 2 + core
    t_r1[slot] = t_s[core]
    for k in range(4):
        for c in range(2):
            cc = (core + c) % 2
            if k or c:
                push(t_s.at[cc], t_r1.at[slot], 23, at_x_core((x + k) % 4, cc))

    def total(ref):
        parts = [ref[i].astype(F32) for i in range(ref.shape[0])]
        while len(parts) > 1:
            parts = [a + b for a, b in zip(parts[::2], parts[1::2])]
        return parts[0]

    arrived(13)
    b_s2[...] = total(b_r1).astype(BF)
    @pl.loop(1, 8)
    def _(k):
        zz = (z8 + k) % 8
        push(b_s2.at[zz % 4], b_r2.at[z8], 24, at_z(zz))
    b_r2[z8] = b_s2[zl]

    arrived(14)
    a_s2[...] = total(a_r1).astype(BF)
    @pl.loop(1, 8)
    def _(k):
        yy = (y + k) % 8
        push(a_s2.at[:, yy], a_r2.at[y], 25, at_y(yy))
    a_r2[y] = a_s2[:, y]

    arrived(23)
    t_r2[y] = total(t_r1)
    @pl.loop(1, 8)
    def _(k):
        push(t_r2.at[y], t_r2.at[y], 26, at_y((y + k) % 8))

    arrived(24)
    b_r3[x] = total(b_r2)
    for k in (1, 3, 2):
        push(b_r3.at[x], b_r3.at[x], 27, at_x(k))

    arrived(25)
    a_s3[...] = total(a_r2).astype(BF)
    @pl.loop(1, 8)
    def _(k):
        zz = (z8 + k) % 8
        push(a_s3.at[zz % 4], a_r3.at[z8], 28, at_z(zz))
    a_r3[z8] = a_s3[zl]

    arrived(26)
    t_r3[z8] = total(t_r2)
    @pl.loop(1, 8)
    def _(k):
        push(t_r3.at[z8], t_r3.at[z8], 29, at_z((z8 + k) % 8))

    arrived(28)
    a_r4[x] = total(a_r3)
    for k in (1, 3, 2):
        push(a_r4.at[x], a_r4.at[x], 30, at_x(k))

    arrived(29)
    t_f[core] = total(t_r3)
    push(t_f.at[core], t_f.at[core], 31, sibling)

    scale = 1.0 / math.sqrt(SEQ * DP * HALF)
    arrived(27)
    pg_ref[:, 512:] = total(b_r3)[:OWN] * scale
    arrived(30)
    for j in range(4):
        pg_ref[:, HALF * j:HALF * (j + 1)] = a_r4[j][:OWN] * scale
    arrived(31)
    for h in range(2):
        for k in range(3):
            tg_ref[k, :, 384 * h:384 * (h + 1)] = t_f[h][2 * k:2 * k + 2] * scale

    finish()


SCRATCH = [
    ((1, C, ROWS), BF),
    ((3, 2, C), F32),
    ((112, C), BF),
    ((1, OWN, SEQ * HALF), BF),
    ((SEQ, PAD, HALF), BF),
    ((SEQ, PAD, HALF), BF),
    ((32, PAD, HALF), BF),
    ((2, DP, 64, C), BF),
    ((2, 96, HALF), BF),
    ((2, 96, HALF), BF),
    ((HALF + 2 * PAD, SEQ * PAD), BF),
    ((C, HALF), F32),
    ((6, C, HALF), F32),
    ((2, C, HALF), F32),
    ((2, C, HALF), F32),
    ((2, C, HALF), F32),
    ((3, C, HALF), F32),
    ((C, ROWS), BF),
    ((C, HALF), BF),
    ((C, HALF), BF),
    ((C, 3 * HALF), BF),
    ((C, 3 * HALF), BF),
    ((C, 6 * HALF), F32),
    ((C, 12 * HALF), BF),
    ((4, 4, 8, PAD, HALF), BF),
    ((4, 4, 8, PAD, HALF), BF),
    ((4, 8, PAD, HALF), BF),
    ((8, 4, PAD, HALF), BF),
    ((4, PAD, HALF), BF),
    ((8, PAD, HALF), BF),
    ((4, PAD, HALF), F32),
    ((4, 8, PAD, 256), BF),
    ((8, 4, PAD, 256), BF),
    ((4, PAD, 256), BF),
    ((8, PAD, 256), BF),
    ((4, PAD, 256), F32),
    ((2, 8, 384), F32),
    ((8, 8, 384), F32),
    ((8, 8, 384), F32),
    ((8, 8, 384), F32),
    ((2, 8, 384), F32),
]


def local(sequence_acts, taps, dilations, left_link, projection, head_cotangent):
    vmem = pl.BlockSpec(memory_space=pltpu.VMEM)
    hbm = pl.BlockSpec(memory_space=pltpu.HBM)
    grad, weight, tap_grads = pl.pallas_call(
        kernel,
        out_shape=(
            jax.ShapeDtypeStruct((1, C, ROWS), BF),
            jax.ShapeDtypeStruct((OWN, C), F32),
            jax.ShapeDtypeStruct((3, 2, C), F32),
        ),
        in_specs=[hbm] * 6,
        out_specs=(vmem, vmem, vmem),
        scratch_shapes=[pltpu.VMEM(shape, kind) for shape, kind in SCRATCH[:4]]
        + [pltpu.SMEM((2,), jnp.int32), pltpu.SMEM((1, SEQ), jnp.int32)]
        + [pltpu.VMEM(shape, kind) for shape, kind in SCRATCH[4:]]
        + [pltpu.SemaphoreType.DMA((44,)), pltpu.SemaphoreType.DMA((44,)), pltpu.SemaphoreType.DMA((6,))],
        compiler_params=pltpu.CompilerParams(
            collective_id=0, has_side_effects=True, vmem_limit_bytes=60 * 1024 * 1024
        ),
        cost_estimate=pl.CostEstimate(
            flops=1_000_000_000, bytes_accessed=4_000_000, transcendentals=600_000
        ),
    )(sequence_acts, jnp.transpose(taps, (2, 0, 1)), dilations, left_link, projection, head_cotangent)
    return grad, weight, jnp.transpose(tap_grads, (1, 2, 0))


def solution(mesh):
    placed = (P("dp", None, "seq"), P(), P(), P("dp", None), P("dp", None), P("dp", "seq", None))
    return jax.shard_map(
        local,
        mesh=mesh,
        in_specs=placed,
        out_specs=(P("dp", None, "seq"), P("seq", None), P()),
        check_vma=False,
    )
```

time: 72.5 us -> 57.1 us (0.79)
  Pallas kernels: 65.3 us -> 53 us
  local copies, waits for them, and re-layouts: 6.21 us -> 3.11 us
    pallas_call x1, Pallas kernels: 65.3 us -> 53 us  [local(): pl.pallas_call(kernel, out_shape=(jax.ShapeDtypeStruct((1, C, ROWS), BF),...]
    unnamed x15 -> x7, local copies, waits for them, and re-layouts: 6.21 us -> 3.11 us
where the time goes in v2:
time: 57.1 us; the launch traced here: 56.8 us
  Pallas kernels  53 us (93%)
  local copies, waits for them, and re-layouts  3.11 us (5%)
  between operations  0.65 us (1%)
    pallas_call x1, Pallas kernels, local(): pl.pallas_call(kernel, out_shape=(jax.ShapeDtypeStruct((1, C, ROWS), BF),...  53 us
    unnamed x7, local copies, waits for them, and re-layouts  3.11 us

profile of v2, /device:TPU:1, one launch (start us, length us, event | category | flops | bytes accessed | tf_op | source)
XLA Modules:
  0.0 56.8 jit_solution(7219374589211163721)
XLA Ops:
  0.6 53.0 %shard_map.85 = (bf16[1,768,256]{2,1,0:T(8,128)(2,1)}, f32[14,768]{1,0:T(8,128)}, f32[3,2,768]{2,1,0:T(2,128)}) custom-call(bf16[1,768,256]{2,1,0:T(8,128)(2,1)} %x_in.1, f32[3,2,768]{2,1,0:T(2,128)} %bitcast.3, s32[2]{0:T(128)} %dil_in.1, s32[1,64]{1,0:T(1,128)} %link_in.1, bf16[112,768]{1,0:T(8,128)(2,1)} %proj_in.1, bf16[1,14,8192]{2,1,0:T(8,128)(2,1)} %cot_in.1), custom_call_target="tpu_custom_call" | custom-call | flops 1000000000 | bytes 4000000 | tf_op jit(solution)/shard_map/pallas_call | solution.py:539
  53.7 0.0 copy-start
  53.7 1.8 %copy.12 = bf16[1,768,256]{2,1,0:T(8,128)(2,1)} copy(bf16[1,768,256]{2,1,0:T(8,128)(2,1)} %get-tuple-element.12) | data formatting | bytes 786432
  55.5 0.0 copy-done
  55.5 0.0 copy-start.1
  55.5 0.6 %copy.13 = f32[14,768]{1,0:T(8,128)} copy(f32[14,768]{1,0:T(8,128)S(1)} %copy-done) | data formatting | bytes 86016
  56.1 0.1 copy-done.1
  56.2 0.6 %copy.14 = f32[2,768,3]{1,0,2:T(2,128)} copy(f32[2,768,3]{1,0,2:T(2,128)S(1)} %bitcast.2) | data formatting | bytes 36864
Async XLA Ops:
  53.7 1.8 %copy-start = (f32[14,768]{1,0:T(8,128)S(1)}, f32[14,768]{1,0:T(8,128)}, u32[]{:S(2)}) copy-start(f32[14,768]{1,0:T(8,128)} %get-tuple-element.13) | copy-start | bytes 129028
  55.5 0.7 %copy-start.1 = (f32[3,2,768]{2,1,0:T(2,128)S(1)}, f32[3,2,768]{2,1,0:T(2,128)}, u32[]{:S(2)}) copy-start(f32[3,2,768]{2,1,0:T(2,128)} %get-tuple-element.8) | copy-start | bytes 55300

commit v3 on v2

--- a/solution.py
+++ b/solution.py
@@ -26,6 +26,7 @@
     range(1, SEQ),
     key=lambda m: -((0, 1, 2, 2)[m >> 4] + (0, 1, 2, 2, 4, 3, 2, 2)[(m >> 1) & 7]),
 )
+FAR_RING = (4, 3, 5, 2, 6, 1, 7)
 GELU = 0.7978845608028654
 
 
@@ -53,13 +54,14 @@
 
 def kernel(
     x_in, taps_in, dil_in, link_in, proj_in, cot_in,
+    out_hbm, pg_hbm, tg_hbm,
     out_ref, pg_ref, tg_ref,
     x_ref, taps_ref, proj_ref, cot_ref, dil_ref, link_ref,
     stage, cot, cot_sib, pfull, edge_s, edge_r, cot_t, halo, wide,
     a0, a1, s0, s1, x2, pooled, pooled_sib, g2, g1, moved, prods,
     a_s1, a_r1, a_s2, a_r2, a_s3, a_r3, a_r4, b_s1, b_r1, b_s2, b_r2, b_r3,
-    t_s, t_r1, t_r2, t_r3, t_f,
-    send, recv, load,
+    t_r1, t_r2, t_r3,
+    send, recv, load, store,
 ):
     s = lax.axis_index("seq")
     d = lax.axis_index("dp")
@@ -86,9 +88,9 @@
     whole = {
         0: edge_s.at[0], 1: edge_s.at[0], 6: stage.at[pl.ds(0, SEQ - 1)], 7: pooled, 12: cot_sib,
         13: b_r1.at[pl.ds(0, 7)], 14: a_r1.at[pl.ds(0, 3)], 21: cot_t.at[pl.ds(0, PAD)], 22: cot_t.at[pl.ds(0, PAD)],
-        23: t_r1.at[pl.ds(0, 7)], 24: b_r2.at[pl.ds(0, 7)], 25: a_r2.at[pl.ds(0, 7)],
-        26: t_r2.at[pl.ds(0, 7)], 27: b_r3.at[pl.ds(0, 3)], 28: a_r3.at[pl.ds(0, 7)],
-        29: t_r3.at[pl.ds(0, 7)], 30: a_r4.at[pl.ds(0, 3)], 31: t_f.at[0],
+        23: t_r1.at[pl.ds(0, 7)], 24: b_r2.at[pl.ds(0, 7)], 25: a_r2.at[pl.ds(0, 7)], 28: a_r3.at[pl.ds(0, 7)],
+        26: t_r2.at[pl.ds(0, 7)], 27: b_r3.at[pl.ds(0, 3)],
+        29: t_r3.at[pl.ds(0, 7)], 30: a_r4.at[pl.ds(0, 3)],
         3: pfull.at[0, pl.ds(0, 3)], 4: pfull.at[0, pl.ds(0, 4)],
     }
     for i in range(4):
@@ -309,8 +311,6 @@
     ).astype(BF)
     push(cot_t.at[pl.ds(HALF - PAD, PAD)], cot_t.at[pl.ds(HALF + PAD, PAD)], 21, {"seq": (s + 1) % SEQ, "dp": d})
     push(cot_t.at[pl.ds(0, PAD)], cot_t.at[pl.ds(HALF, PAD)], 22, {"seq": (s + SEQ - 1) % SEQ, "dp": d})
-    pass_core(0)
-    pass_core(1)
     arrived(7)
     arrived(12)
     mine = cot[pl.ds(core * 32, 32)].reshape(512, HALF)
@@ -334,8 +334,8 @@
     b_r1[y] = b_s1[:, y]
     a_r1[x] = a_s1[x]
 
-    pass_core(2)
-    pass_core(3)
+    for i in range(4):
+        pass_core(i)
     for i in (4, SIB_PART, SIB_PART + 1, SIB_PART + 2, SIB_PART + 3, 21, 22):
         arrived(i)
     back = jnp.dot(cot_t[...], pfull[...].reshape(SEQ * PAD, C), preferred_element_type=F32)
@@ -404,19 +404,22 @@
         for k, part in enumerate((hi, g, lo)):
             keep_product(rows, 2 * k, a0[0, rows, :] * part[0] + a0[1, rows, :] * part[1])
 
+    stores = [
+        pltpu.make_async_copy(a, b, store.at[i])
+        for i, (a, b) in enumerate(((out_ref, out_hbm), (pg_ref, pg_hbm), (tg_ref, tg_hbm)))
+    ]
+    stores[0].start()
     which = lax.broadcasted_iota(jnp.int32, (8, 12 * HALF), 1) // HALF
     row = lax.broadcasted_iota(jnp.int32, (8, 12 * HALF), 0)
     ones = jnp.where(which % 6 == row, 1.0, 0.0).astype(BF)
     flat = lax.dot_general(ones, prods[...], nt, preferred_element_type=F32)
-    t_s[0] = flat[:, :384]
-    t_s[1] = flat[:, 384:]
     slot = x * 2 + core
-    t_r1[slot] = t_s[core]
-    for k in range(4):
-        for c in range(2):
-            cc = (core + c) % 2
-            if k or c:
-                push(t_s.at[cc], t_r1.at[slot], 23, at_x_core((x + k) % 4, cc))
+    t_r1[slot] = jnp.concatenate([flat[:, :384], flat[:, 384:]], axis=0).astype(BF)
+    for k in (2, 1, 3, 0):
+        for cc in range(2):
+            if k:
+                push(t_r1.at[slot], t_r1.at[slot], 23, at_x_core((x + k) % 4, cc))
+    push(t_r1.at[slot], t_r1.at[slot], 23, sibling)
 
     def total(ref):
         parts = [ref[i].astype(F32) for i in range(ref.shape[0])]
@@ -426,25 +429,22 @@
 
     arrived(13)
     b_s2[...] = total(b_r1).astype(BF)
-    @pl.loop(1, 8)
-    def _(k):
+    for k in FAR_RING:
         zz = (z8 + k) % 8
         push(b_s2.at[zz % 4], b_r2.at[z8], 24, at_z(zz))
     b_r2[z8] = b_s2[zl]
 
     arrived(14)
     a_s2[...] = total(a_r1).astype(BF)
-    @pl.loop(1, 8)
-    def _(k):
+    for k in FAR_RING:
         yy = (y + k) % 8
         push(a_s2.at[:, yy], a_r2.at[y], 25, at_y(yy))
     a_r2[y] = a_s2[:, y]
 
     arrived(23)
-    t_r2[y] = total(t_r1)
-    @pl.loop(1, 8)
-    def _(k):
-        push(t_r2.at[y], t_r2.at[y], 26, at_y((y + k) % 8))
+    t_r2[z8] = total(t_r1).astype(BF)
+    for k in FAR_RING:
+        push(t_r2.at[z8], t_r2.at[z8], 26, at_z((z8 + k) % 8))
 
     arrived(24)
     b_r3[x] = total(b_r2)
@@ -453,26 +453,23 @@
 
     arrived(25)
     a_s3[...] = total(a_r2).astype(BF)
-    @pl.loop(1, 8)
-    def _(k):
+    for k in FAR_RING:
         zz = (z8 + k) % 8
         push(a_s3.at[zz % 4], a_r3.at[z8], 28, at_z(zz))
     a_r3[z8] = a_s3[zl]
 
     arrived(26)
-    t_r3[z8] = total(t_r2)
-    @pl.loop(1, 8)
-    def _(k):
-        push(t_r3.at[z8], t_r3.at[z8], 29, at_z((z8 + k) % 8))
+    t_r3[y] = total(t_r2).astype(BF)
+    for k in FAR_RING:
+        push(t_r3.at[y], t_r3.at[y], 29, at_y((y + k) % 8))
 
     arrived(28)
     a_r4[x] = total(a_r3)
-    for k in (1, 3, 2):
+    for k in (2, 1, 3):
         push(a_r4.at[x], a_r4.at[x], 30, at_x(k))
 
     arrived(29)
-    t_f[core] = total(t_r3)
-    push(t_f.at[core], t_f.at[core], 31, sibling)
+    taps_total = total(t_r3)
 
     scale = 1.0 / math.sqrt(SEQ * DP * HALF)
     arrived(27)
@@ -480,15 +477,34 @@
     arrived(30)
     for j in range(4):
         pg_ref[:, HALF * j:HALF * (j + 1)] = a_r4[j][:OWN] * scale
-    arrived(31)
     for h in range(2):
         for k in range(3):
-            tg_ref[k, :, 384 * h:384 * (h + 1)] = t_f[h][2 * k:2 * k + 2] * scale
-
+            tg_ref[k, :, 384 * h:384 * (h + 1)] = taps_total[8 * h + 2 * k:8 * h + 2 * k + 2] * scale
+
+    stores[1].start()
+    stores[2].start()
     finish()
+    for copy in stores:
+        copy.wait()
+
+
+def hand_over(*refs):
+    held, sems = refs[6:9], refs[9]
+    loads = [pltpu.make_async_copy(refs[i], held[i], sems.at[i]) for i in range(3)]
+    stores = [pltpu.make_async_copy(held[i], refs[3 + i], sems.at[3 + i]) for i in range(3)]
+    for copy in loads:
+        copy.start()
+    for load, store in zip(loads, stores):
+        load.wait()
+        store.start()
+    for copy in stores:
+        copy.wait()
 
 
 SCRATCH = [
+    ((1, C, ROWS), BF),
+    ((OWN, C), F32),
+    ((3, 2, C), F32),
     ((1, C, ROWS), BF),
     ((3, 2, C), F32),
     ((112, C), BF),
@@ -525,30 +541,28 @@
     ((4, PAD, 256), BF),
     ((8, PAD, 256), BF),
     ((4, PAD, 256), F32),
-    ((2, 8, 384), F32),
-    ((8, 8, 384), F32),
-    ((8, 8, 384), F32),
-    ((8, 8, 384), F32),
-    ((2, 8, 384), F32),
+    ((8, PAD, 384), BF),
+    ((8, PAD, 384), BF),
+    ((8, PAD, 384), BF),
 ]
 
 
 def local(sequence_acts, taps, dilations, left_link, projection, head_cotangent):
-    vmem = pl.BlockSpec(memory_space=pltpu.VMEM)
     hbm = pl.BlockSpec(memory_space=pltpu.HBM)
-    grad, weight, tap_grads = pl.pallas_call(
+    results = (
+        jax.ShapeDtypeStruct((1, C, ROWS), BF),
+        jax.ShapeDtypeStruct((OWN, C), F32),
+        jax.ShapeDtypeStruct((3, 2, C), F32),
+    )
+    parts = pl.pallas_call(
         kernel,
-        out_shape=(
-            jax.ShapeDtypeStruct((1, C, ROWS), BF),
-            jax.ShapeDtypeStruct((OWN, C), F32),
-            jax.ShapeDtypeStruct((3, 2, C), F32),
-        ),
+        out_shape=results,
         in_specs=[hbm] * 6,
-        out_specs=(vmem, vmem, vmem),
-        scratch_shapes=[pltpu.VMEM(shape, kind) for shape, kind in SCRATCH[:4]]
+        out_specs=(hbm, hbm, hbm),
+        scratch_shapes=[pltpu.VMEM(shape, kind) for shape, kind in SCRATCH[:7]]
         + [pltpu.SMEM((2,), jnp.int32), pltpu.SMEM((1, SEQ), jnp.int32)]
-        + [pltpu.VMEM(shape, kind) for shape, kind in SCRATCH[4:]]
-        + [pltpu.SemaphoreType.DMA((44,)), pltpu.SemaphoreType.DMA((44,)), pltpu.SemaphoreType.DMA((6,))],
+        + [pltpu.VMEM(shape, kind) for shape, kind in SCRATCH[7:]]
+        + [pltpu.SemaphoreType.DMA((44,)), pltpu.SemaphoreType.DMA((44,)), pltpu.SemaphoreType.DMA((6,)), pltpu.SemaphoreType.DMA((3,))],
         compiler_params=pltpu.CompilerParams(
             collective_id=0, has_side_effects=True, vmem_limit_bytes=60 * 1024 * 1024
         ),
@@ -556,6 +570,15 @@
             flops=1_000_000_000, bytes_accessed=4_000_000, transcendentals=600_000
         ),
     )(sequence_acts, jnp.transpose(taps, (2, 0, 1)), dilations, left_link, projection, head_cotangent)
+    grad, weight, tap_grads = pl.pallas_call(
+        hand_over,
+        out_shape=results,
+        in_specs=[hbm] * 3,
+        out_specs=(hbm,) * 3,
+        scratch_shapes=[pltpu.VMEM(shape, kind) for shape, kind in SCRATCH[:3]]
+        + [pltpu.SemaphoreType.DMA((6,))],
+        compiler_params=pltpu.CompilerParams(vmem_limit_bytes=60 * 1024 * 1024),
+    )(*parts)
     return grad, weight, jnp.transpose(tap_grads, (1, 2, 0))
 
 

time: 57.1 us -> 53.1 us (0.930)
  local copies, waits for them, and re-layouts: 3.11 us -> 0 us
  Pallas kernels: 53 us -> 52.2 us
    unnamed x7 -> x0, local copies, waits for them, and re-layouts: 3.11 us -> none
    pallas_call x1 -> x2, Pallas kernels: 53 us -> 52.2 us  [the longest x1 50.4 us: local(): pl.pallas_call(kernel, out_shape=results, in_specs=[hbm] * 6, out_specs=(...]
where the time goes in v3:
time: 53.1 us; the launch traced here: 52.8 us
  Pallas kernels  52.2 us (98%)
  between operations  0.64 us (1%)
    pallas_call x1, Pallas kernels, local(): pl.pallas_call(kernel, out_shape=results, in_specs=[hbm] * 6, out_specs=(...  50.4 us
    pallas_call x1, Pallas kernels, local(): pl.pallas_call(hand_over, out_shape=results, in_specs=[hbm] * 3, out_spec...  1.8 us

profile of v3, /device:TPU:1, one launch (start us, length us, event | category | flops | bytes accessed | tf_op | source)
XLA Modules:
  0.0 52.8 jit_solution(4966218260816159894)
XLA Ops:
  0.6 50.4 %shard_map.85 = (bf16[1,768,256]{2,1,0:T(8,128)(2,1)}, f32[14,768]{1,0:T(8,128)}, f32[3,2,768]{2,1,0:T(2,128)}) custom-call(bf16[1,768,256]{2,1,0:T(8,128)(2,1)} %x_in.1, f32[3,2,768]{2,1,0:T(2,128)} %bitcast.2, s32[2]{0:T(128)} %dil_in.1, s32[1,64]{1,0:T(1,128)} %link_in.1, bf16[112,768]{1,0:T(8,128)(2,1)} %proj_in.1, bf16[1,14,8192]{2,1,0:T(8,128)(2,1)} %cot_in.1), custom_call_target="tpu_custom_call" | custom-call | flops 1000000000 | bytes 4000000 | tf_op jit(solution)/shard_map/pallas_call | solution.py:557
  51.0 1.8 %shard_map.86 = (bf16[1,768,256]{2,1,0:T(8,128)(2,1)}, f32[14,768]{1,0:T(8,128)}, f32[3,2,768]{2,1,0:T(2,128)}) custom-call(bf16[1,768,256]{2,1,0:T(8,128)(2,1)} %get-tuple-element.9.refs_0_, f32[14,768]{1,0:T(8,128)} %get-tuple-element.10.refs_1_, f32[3,2,768]{2,1,0:T(2,128)} %get-tuple-element.11.refs_2_), custom_call_target="tpu_custom_call" | custom-call | tf_op jit(solution)/shard_map/pallas_call | solution.py:573

commit v4 on v3

--- a/solution.py
+++ b/solution.py
@@ -24,7 +24,7 @@
 Z_PART, X_PART, SIB_PART = 32, 36, 40
 FAR_FIRST = sorted(
     range(1, SEQ),
-    key=lambda m: -((0, 1, 2, 2)[m >> 4] + (0, 1, 2, 2, 4, 3, 2, 2)[(m >> 1) & 7]),
+    key=lambda m: -100 * (m & 1) - ((0, 1, 2, 2)[m >> 4] + (0, 1, 2, 2, 4, 3, 2, 2)[(m >> 1) & 7]),
 )
 FAR_RING = (4, 3, 5, 2, 6, 1, 7)
 GELU = 0.7978845608028654
@@ -54,14 +54,13 @@
 
 def kernel(
     x_in, taps_in, dil_in, link_in, proj_in, cot_in,
-    out_hbm, pg_hbm, tg_hbm,
     out_ref, pg_ref, tg_ref,
     x_ref, taps_ref, proj_ref, cot_ref, dil_ref, link_ref,
     stage, cot, cot_sib, pfull, edge_s, edge_r, cot_t, halo, wide,
-    a0, a1, s0, s1, x2, pooled, pooled_sib, g2, g1, moved, prods,
+    a0, a1, s0, s1, x2, pooled, pooled_sib, g2, g1, moved, prods, unit, halves, spread, matrix1, matrix0, pick_taps,
     a_s1, a_r1, a_s2, a_r2, a_s3, a_r3, a_r4, b_s1, b_r1, b_s2, b_r2, b_r3,
     t_r1, t_r2, t_r3,
-    send, recv, load, store,
+    send, recv, load,
 ):
     s = lax.axis_index("seq")
     d = lax.axis_index("dp")
@@ -86,7 +85,7 @@
         return {"seq": (zz % 4) * 16 + y * 2 + core, "dp": (zz // 4) * 4 + x}
 
     whole = {
-        0: edge_s.at[0], 1: edge_s.at[0], 6: stage.at[pl.ds(0, SEQ - 1)], 7: pooled, 12: cot_sib,
+        0: edge_s.at[0], 1: edge_s.at[0], 2: stage.at[pl.ds(0, 32)], 6: stage.at[pl.ds(0, 31)], 7: pooled, 12: cot_sib,
         13: b_r1.at[pl.ds(0, 7)], 14: a_r1.at[pl.ds(0, 3)], 21: cot_t.at[pl.ds(0, PAD)], 22: cot_t.at[pl.ds(0, PAD)],
         23: t_r1.at[pl.ds(0, 7)], 24: b_r2.at[pl.ds(0, 7)], 25: a_r2.at[pl.ds(0, 7)], 28: a_r3.at[pl.ds(0, 7)],
         26: t_r2.at[pl.ds(0, 7)], 27: b_r3.at[pl.ds(0, 3)],
@@ -140,9 +139,6 @@
             )
         )
     ]
-    for copy in loads:
-        copy.start()
-
     barrier = pltpu.get_barrier_semaphore()
 
     def greet(where):
@@ -157,6 +153,9 @@
     for k in range(1, 4):
         greet(at_x(k))
         greet({"seq": sib, "dp": zh * 4 + (x + k) % 4})
+
+    for copy in loads:
+        copy.start()
 
     lane = lax.broadcasted_iota(jnp.int32, (1, HALF), 1)
 
@@ -201,6 +200,50 @@
     pick = jnp.where((inner < OWN) & (source == col), 1.0, 0.0).astype(BF)
     pfull[core, d] = jnp.dot(pick, proj_ref[...], preferred_element_type=F32).astype(BF)
 
+    for copy in loads[3:]:
+        copy.wait()
+    left_linked = link_ref[0, s] >= 0
+    right_linked = link_ref[0, (s + 1) % SEQ] >= 0
+    six = jnp.concatenate([taps_ref[k] for k in range(3)] + [jnp.zeros((2, C), F32)], axis=0)
+    six = jnp.transpose(six)
+    for i in range(6):
+        wide[i] = jnp.broadcast_to(six[:, i:i + 1], (C, HALF))
+    d0 = dil_ref[0]
+
+
+    unit[...] = jnp.where(
+        lax.broadcasted_iota(jnp.int32, (HALF, HALF), 0) == lax.broadcasted_iota(jnp.int32, (HALF, HALF), 1),
+        1.0, 0.0,
+    ).astype(BF)
+    two = lax.broadcasted_iota(jnp.int32, (ROWS, HALF), 0) // 2
+    pair = two == lax.broadcasted_iota(jnp.int32, (ROWS, HALF), 1)
+    halves[...] = jnp.where(pair, 0.5, 0.0).astype(BF)
+    ring = 3 * HALF
+    shape = (HALF + 2 * PAD, ring)
+    at = lax.broadcasted_iota(jnp.int32, shape, 0)
+    to = lax.broadcasted_iota(jnp.int32, shape, 1)
+    right = (to >= ROWS) & (to < ROWS + 16) & right_linked
+    left = (to >= ring - 16) & left_linked
+    origin = jnp.where(
+        to < ROWS, to // 2,
+        jnp.where(right, HALF + (to - ROWS) // 2, jnp.where(left, HALF + 24 + (to - ring + 16) // 2, -1)),
+    )
+    spread[...] = jnp.where(at == origin, 1.0, 0.0).astype(BF)
+
+    def shifts(dist, length):
+        at = lax.broadcasted_iota(jnp.int32, (ring, 2 * length), 0)
+        to = lax.broadcasted_iota(jnp.int32, (ring, 2 * length), 1)
+        low = to < length
+        to = jnp.where(low, to - dist + ring, to - length + dist)
+        to = jnp.where(to >= ring, to - ring, to)
+        return jnp.where(at == to, 1.0, 0.0).astype(BF)
+
+    matrix1[...] = shifts(LAST_DILATION, ring)
+    matrix0[...] = shifts(d0, ROWS)
+    which = lax.broadcasted_iota(jnp.int32, (8, 12 * HALF), 1) // HALF
+    row = lax.broadcasted_iota(jnp.int32, (8, 12 * HALF), 0)
+    pick_taps[...] = jnp.where(which % 6 == row, 1.0, 0.0).astype(BF)
+
     pl.semaphore_wait(barrier, SEQ - 1 + 4 + 6)
 
     push(edge_s.at[0], edge_r.at[0], 0, {"seq": (s + 1) % SEQ, "dp": d})
@@ -212,6 +255,13 @@
                 rows = pfull.at[core, d, pl.ds(PAD * i, PAD)]
                 for far in (2, 1):
                     push(rows, rows, Z_PART + i, at_z((z8 + 8 + far * step) % 8))
+    me = core * 32 + zl * 8 + y
+    for m in FAR_FIRST:
+        t = s ^ m
+        push(stage.at[t], cot.at[me], 2 if m & 1 else 6, {"seq": t, "dp": d})
+
+    cot[me] = stage[s]
+
     for k in (2, 1, 3):
         push(pfull.at[core, d], pfull.at[core, d], 3, at_x(k))
     other = (1 - zh) * 4
@@ -226,23 +276,6 @@
         arrived(X_PART + i)
         rows = pfull.at[core, pl.ds(other, 4), pl.ds(PAD * i, PAD)]
         push(rows, rows, SIB_PART + i, sibling)
-
-    me = core * 32 + zl * 8 + y
-    for m in FAR_FIRST:
-        t = s ^ m
-        push(stage.at[t], cot.at[me], 6, {"seq": t, "dp": d})
-
-    cot[me] = stage[s]
-
-    for copy in loads[3:]:
-        copy.wait()
-    left_linked = link_ref[0, s] >= 0
-    right_linked = link_ref[0, (s + 1) % SEQ] >= 0
-    six = jnp.concatenate([taps_ref[k] for k in range(3)] + [jnp.zeros((2, C), F32)], axis=0)
-    six = jnp.transpose(six)
-    for i in range(6):
-        wide[i] = jnp.broadcast_to(six[:, i:i + 1], (C, HALF))
-    d0 = dil_ref[0]
 
     def weights(rows):
         return [[wide[2 * k + b, rows, :] for k in range(3)] for b in range(2)]
@@ -284,29 +317,20 @@
                 v = ones[j] + ((w[1][0] * lo[j] + w[1][1] * acts1[j]) + w[1][2] * hi[j])
                 x2[rows, HALF * j:HALF * (j + 1)] = v.astype(BF)
 
-    forward(0, 4)
+    forward(0, 6)
     pass_x(0)
-    forward(4, 8)
     pass_x(1)
+    forward(6, 12)
+    pooled[...] = jnp.dot(x2[...], halves[...], preferred_element_type=F32).astype(BF)
+    push(pooled, pooled_sib, 7, {"seq": sib, "dp": d})
     pass_x(2)
-    forward(8, 12)
     pass_x(3)
-    arrived(3)
-    rows = pfull.at[core, pl.ds(zh * 4, 4)]
-    push(rows, rows, 4, sibling)
-
-    two = lax.broadcasted_iota(jnp.int32, (ROWS, HALF), 0) // 2
-    pair = two == lax.broadcasted_iota(jnp.int32, (ROWS, HALF), 1)
-    halves = jnp.where(pair, 0.5, 0.0).astype(BF)
-    pooled[...] = jnp.dot(x2[...], halves, preferred_element_type=F32).astype(BF)
-    push(pooled, pooled_sib, 7, {"seq": sib, "dp": d})
-
+    arrived(2)
+    push(cot.at[pl.ds((1 - core) * 32, 32)], cot_sib, 12, sibling)
     arrived(6)
-    push(cot.at[pl.ds((1 - core) * 32, 32)], cot_sib, 12, sibling)
-    eye = lax.broadcasted_iota(jnp.int32, (HALF, HALF), 0) == lax.broadcasted_iota(jnp.int32, (HALF, HALF), 1)
     nt = (((1,), (1,)), ((), ()))
     cot_t[:HALF] = lax.dot_general(
-        jnp.where(eye, 1.0, 0.0).astype(BF), cot[...].reshape(SEQ * PAD, HALF), nt,
+        unit[...], cot[...].reshape(SEQ * PAD, HALF), nt,
         preferred_element_type=F32,
     ).astype(BF)
     push(cot_t.at[pl.ds(HALF - PAD, PAD)], cot_t.at[pl.ds(HALF + PAD, PAD)], 21, {"seq": (s + 1) % SEQ, "dp": d})
@@ -315,53 +339,37 @@
     arrived(12)
     mine = cot[pl.ds(core * 32, 32)].reshape(512, HALF)
     theirs = cot_sib[...].reshape(512, HALF)
-    for j in (2, 0, 1):
+    for j in range(3):
         cols = pl.ds(256 * j, 256)
         part = lax.dot_general(mine, pooled[cols, :], nt, preferred_element_type=F32)
         part = part + lax.dot_general(theirs, pooled_sib[cols, :], nt, preferred_element_type=F32)
         part = part.astype(BF)
         if j == 2:
             b_s1[...] = part.reshape(4, 8, PAD, 256)
-            @pl.loop(1, 8)
-            def _(k):
+            for k in FAR_RING:
                 yy = (y + k) % 8
                 push(b_s1.at[:, yy], b_r1.at[y], 13, at_y(yy))
         else:
             a_s1[2 * j] = part[:, :HALF].reshape(4, 8, PAD, HALF)
             a_s1[2 * j + 1] = part[:, HALF:].reshape(4, 8, PAD, HALF)
-    for k in (1, 3, 2):
-        push(a_s1.at[(x + k) % 4], a_r1.at[x], 14, at_x(k))
+        if j == 1:
+            for k in (2, 1, 3):
+                push(a_s1.at[(x + k) % 4], a_r1.at[x], 14, at_x(k))
     b_r1[y] = b_s1[:, y]
     a_r1[x] = a_s1[x]
 
+    arrived(3)
+    rows = pfull.at[core, pl.ds(zh * 4, 4)]
+    push(rows, rows, 4, sibling)
     for i in range(4):
         pass_core(i)
     for i in (4, SIB_PART, SIB_PART + 1, SIB_PART + 2, SIB_PART + 3, 21, 22):
         arrived(i)
     back = jnp.dot(cot_t[...], pfull[...].reshape(SEQ * PAD, C), preferred_element_type=F32)
     back = (0.5 * back).astype(BF)
-    ring = 3 * HALF
-    shape = (HALF + 2 * PAD, ring)
-    at = lax.broadcasted_iota(jnp.int32, shape, 0)
-    to = lax.broadcasted_iota(jnp.int32, shape, 1)
-    right = (to >= ROWS) & (to < ROWS + 16) & right_linked
-    left = (to >= ring - 16) & left_linked
-    origin = jnp.where(
-        to < ROWS, to // 2,
-        jnp.where(right, HALF + (to - ROWS) // 2, jnp.where(left, HALF + 24 + (to - ring + 16) // 2, -1)),
-    )
-    spread = jnp.where(at == origin, 1.0, 0.0).astype(BF)
     g2[...] = lax.dot_general(
-        back, spread, (((0,), (0,)), ((), ())), preferred_element_type=F32
+        back, spread[...], (((0,), (0,)), ((), ())), preferred_element_type=F32
     ).astype(BF)
-
-    def shifts(dist, length):
-        at = lax.broadcasted_iota(jnp.int32, (ring, 2 * length), 0)
-        to = lax.broadcasted_iota(jnp.int32, (ring, 2 * length), 1)
-        low = to < length
-        to = jnp.where(low, to - dist + ring, to - length + dist)
-        to = jnp.where(to >= ring, to - ring, to)
-        return jnp.where(at == to, 1.0, 0.0).astype(BF)
 
     def keep_product(rows, column, total):
         high = total.astype(BF)
@@ -369,9 +377,7 @@
         low = (total - high.astype(F32)).astype(BF)
         prods[rows, HALF * (column + 6):HALF * (column + 7)] = low
 
-    matrix1 = shifts(LAST_DILATION, ring)
-    matrix0 = shifts(d0, ROWS)
-    moved[...] = jnp.dot(g2[...], matrix1, preferred_element_type=F32)
+    moved[...] = jnp.dot(g2[...], matrix1[...], preferred_element_type=F32)
 
     @pl.loop(0, C // SLAB)
     def _(i):
@@ -389,30 +395,21 @@
         for k, part in enumerate((hi, g, lo)):
             keep_product(rows, 2 * k + 1, a1[0, rows, :] * part[0] + a1[1, rows, :] * part[1])
 
-    moved[:, :2 * ROWS] = jnp.dot(g1[...], matrix0, preferred_element_type=F32)
+    moved[:, :2 * ROWS] = jnp.dot(g1[...], matrix0[...], preferred_element_type=F32)
+
+    def around(rows):
+        g = [g1[rows, HALF * j:HALF * (j + 1)].astype(F32) for j in range(2)]
+        lo = [moved[rows, HALF * j:HALF * (j + 1)] for j in range(2)]
+        hi = [moved[rows, ROWS + HALF * j:ROWS + HALF * (j + 1)] for j in range(2)]
+        return hi, g, lo
 
     @pl.loop(0, C // SLAB)
     def _(i):
         rows = pl.ds(pl.multiple_of(i * SLAB, SLAB), SLAB)
-        w = weights(rows)[0]
-        g = [g1[rows, HALF * j:HALF * (j + 1)].astype(F32) for j in range(2)]
-        lo = [moved[rows, HALF * j:HALF * (j + 1)] for j in range(2)]
-        hi = [moved[rows, ROWS + HALF * j:ROWS + HALF * (j + 1)] for j in range(2)]
-        for j in range(2):
-            conv = (w[0] * hi[j] + w[1] * g[j]) + w[2] * lo[j]
-            out_ref[0, rows, HALF * j:HALF * (j + 1)] = (g[j] + conv * s0[j, rows, :]).astype(BF)
-        for k, part in enumerate((hi, g, lo)):
+        for k, part in enumerate(around(rows)):
             keep_product(rows, 2 * k, a0[0, rows, :] * part[0] + a0[1, rows, :] * part[1])
 
-    stores = [
-        pltpu.make_async_copy(a, b, store.at[i])
-        for i, (a, b) in enumerate(((out_ref, out_hbm), (pg_ref, pg_hbm), (tg_ref, tg_hbm)))
-    ]
-    stores[0].start()
-    which = lax.broadcasted_iota(jnp.int32, (8, 12 * HALF), 1) // HALF
-    row = lax.broadcasted_iota(jnp.int32, (8, 12 * HALF), 0)
-    ones = jnp.where(which % 6 == row, 1.0, 0.0).astype(BF)
-    flat = lax.dot_general(ones, prods[...], nt, preferred_element_type=F32)
+    flat = lax.dot_general(pick_taps[...], prods[...], nt, preferred_element_type=F32)
     slot = x * 2 + core
     t_r1[slot] = jnp.concatenate([flat[:, :384], flat[:, 384:]], axis=0).astype(BF)
     for k in (2, 1, 3, 0):
@@ -421,11 +418,27 @@
                 push(t_r1.at[slot], t_r1.at[slot], 23, at_x_core((x + k) % 4, cc))
     push(t_r1.at[slot], t_r1.at[slot], 23, sibling)
 
+    @pl.loop(0, C // SLAB)
+    def _(i):
+        rows = pl.ds(pl.multiple_of(i * SLAB, SLAB), SLAB)
+        w = weights(rows)[0]
+        hi, g, lo = around(rows)
+        for j in range(2):
+            conv = (w[0] * hi[j] + w[1] * g[j]) + w[2] * lo[j]
+            out_ref[0, rows, HALF * j:HALF * (j + 1)] = (g[j] + conv * s0[j, rows, :]).astype(BF)
+
     def total(ref):
         parts = [ref[i].astype(F32) for i in range(ref.shape[0])]
         while len(parts) > 1:
             parts = [a + b for a, b in zip(parts[::2], parts[1::2])]
         return parts[0]
+
+    arrived(14)
+    a_s2[...] = total(a_r1).astype(BF)
+    for k in FAR_RING:
+        yy = (y + k) % 8
+        push(a_s2.at[:, yy], a_r2.at[y], 25, at_y(yy))
+    a_r2[y] = a_s2[:, y]
 
     arrived(13)
     b_s2[...] = total(b_r1).astype(BF)
@@ -434,22 +447,10 @@
         push(b_s2.at[zz % 4], b_r2.at[z8], 24, at_z(zz))
     b_r2[z8] = b_s2[zl]
 
-    arrived(14)
-    a_s2[...] = total(a_r1).astype(BF)
-    for k in FAR_RING:
-        yy = (y + k) % 8
-        push(a_s2.at[:, yy], a_r2.at[y], 25, at_y(yy))
-    a_r2[y] = a_s2[:, y]
-
     arrived(23)
     t_r2[z8] = total(t_r1).astype(BF)
     for k in FAR_RING:
         push(t_r2.at[z8], t_r2.at[z8], 26, at_z((z8 + k) % 8))
-
-    arrived(24)
-    b_r3[x] = total(b_r2)
-    for k in (1, 3, 2):
-        push(b_r3.at[x], b_r3.at[x], 27, at_x(k))
 
     arrived(25)
     a_s3[...] = total(a_r2).astype(BF)
@@ -457,6 +458,11 @@
         zz = (z8 + k) % 8
         push(a_s3.at[zz % 4], a_r3.at[z8], 28, at_z(zz))
     a_r3[z8] = a_s3[zl]
+
+    arrived(24)
+    b_r3[x] = total(b_r2)
+    for k in (1, 3, 2):
+        push(b_r3.at[x], b_r3.at[x], 27, at_x(k))
 
     arrived(26)
     t_r3[y] = total(t_r2).astype(BF)
@@ -481,30 +487,19 @@
         for k in range(3):
             tg_ref[k, :, 384 * h:384 * (h + 1)] = taps_total[8 * h + 2 * k:8 * h + 2 * k + 2] * scale
 
-    stores[1].start()
-    stores[2].start()
     finish()
-    for copy in stores:
+
+
+def hand_over(*refs):
+    sems = refs[6]
+    copies = [pltpu.make_async_copy(refs[i], refs[3 + i], sems.at[i]) for i in range(3)]
+    for copy in copies:
+        copy.start()
+    for copy in copies:
         copy.wait()
 
 
-def hand_over(*refs):
-    held, sems = refs[6:9], refs[9]
-    loads = [pltpu.make_async_copy(refs[i], held[i], sems.at[i]) for i in range(3)]
-    stores = [pltpu.make_async_copy(held[i], refs[3 + i], sems.at[3 + i]) for i in range(3)]
-    for copy in loads:
-        copy.start()
-    for load, store in zip(loads, stores):
-        load.wait()
-        store.start()
-    for copy in stores:
-        copy.wait()
-
-
 SCRATCH = [
-    ((1, C, ROWS), BF),
-    ((OWN, C), F32),
-    ((3, 2, C), F32),
     ((1, C, ROWS), BF),
     ((3, 2, C), F32),
     ((112, C), BF),
@@ -529,6 +524,12 @@
     ((C, 3 * HALF), BF),
     ((C, 6 * HALF), F32),
     ((C, 12 * HALF), BF),
+    ((HALF, HALF), BF),
+    ((ROWS, HALF), BF),
+    ((HALF + 2 * PAD, 3 * HALF), BF),
+    ((3 * HALF, 6 * HALF), BF),
+    ((3 * HALF, 4 * HALF), BF),
+    ((8, 12 * HALF), BF),
     ((4, 4, 8, PAD, HALF), BF),
     ((4, 4, 8, PAD, HALF), BF),
     ((4, 8, PAD, HALF), BF),
@@ -549,6 +550,7 @@
 
 def local(sequence_acts, taps, dilations, left_link, projection, head_cotangent):
     hbm = pl.BlockSpec(memory_space=pltpu.HBM)
+    vmem = pl.BlockSpec(memory_space=pltpu.VMEM)
     results = (
         jax.ShapeDtypeStruct((1, C, ROWS), BF),
         jax.ShapeDtypeStruct((OWN, C), F32),
@@ -556,13 +558,13 @@
     )
     parts = pl.pallas_call(
         kernel,
-        out_shape=results,
+        out_shape=tuple(pltpu.VMEM(r.shape, r.dtype) for r in results),
         in_specs=[hbm] * 6,
-        out_specs=(hbm, hbm, hbm),
-        scratch_shapes=[pltpu.VMEM(shape, kind) for shape, kind in SCRATCH[:7]]
+        out_specs=(vmem,) * 3,
+        scratch_shapes=[pltpu.VMEM(shape, kind) for shape, kind in SCRATCH[:4]]
         + [pltpu.SMEM((2,), jnp.int32), pltpu.SMEM((1, SEQ), jnp.int32)]
-        + [pltpu.VMEM(shape, kind) for shape, kind in SCRATCH[7:]]
-        + [pltpu.SemaphoreType.DMA((44,)), pltpu.SemaphoreType.DMA((44,)), pltpu.SemaphoreType.DMA((6,)), pltpu.SemaphoreType.DMA((3,))],
+        + [pltpu.VMEM(shape, kind) for shape, kind in SCRATCH[4:]]
+        + [pltpu.SemaphoreType.DMA((44,)), pltpu.SemaphoreType.DMA((44,)), pltpu.SemaphoreType.DMA((6,))],
         compiler_params=pltpu.CompilerParams(
             collective_id=0, has_side_effects=True, vmem_limit_bytes=60 * 1024 * 1024
         ),
@@ -573,11 +575,10 @@
     grad, weight, tap_grads = pl.pallas_call(
         hand_over,
         out_shape=results,
-        in_specs=[hbm] * 3,
+        in_specs=[vmem] * 3,
         out_specs=(hbm,) * 3,
-        scratch_shapes=[pltpu.VMEM(shape, kind) for shape, kind in SCRATCH[:3]]
-        + [pltpu.SemaphoreType.DMA((6,))],
-        compiler_params=pltpu.CompilerParams(vmem_limit_bytes=60 * 1024 * 1024),
+        scratch_shapes=[pltpu.SemaphoreType.DMA((3,))],
+        compiler_params=pltpu.CompilerParams(vmem_limit_bytes=16 * 1024 * 1024),
     )(*parts)
     return grad, weight, jnp.transpose(tap_grads, (1, 2, 0))
 

time: 53.1 us -> 49.7 us (0.936)
  Pallas kernels: 52.2 us -> 49 us
    pallas_call x2, Pallas kernels: 52.2 us -> 49 us  [the longest x1 48.2 us: local(): pl.pallas_call(kernel, out_shape=tuple((pltpu.VMEM(r.shape, r.dtype) for...]
where the time goes in v4:
time: 49.7 us; the launch traced here: 49.6 us
  Pallas kernels  49 us (99%)
  between operations  0.64 us (1%)
    pallas_call x1, Pallas kernels, local(): pl.pallas_call(kernel, out_shape=tuple((pltpu.VMEM(r.shape, r.dtype) for...  48.2 us

profile of v4, /device:TPU:1, one launch (start us, length us, event | category | flops | bytes accessed | tf_op | source)
XLA Modules:
  0.0 49.6 jit_solution(605047454509935449)
XLA Ops:
  0.6 48.2 %shard_map.85 = (bf16[1,768,256]{2,1,0:T(8,128)(2,1)S(1)}, f32[14,768]{1,0:T(8,128)S(1)}, f32[3,2,768]{2,1,0:T(2,128)S(1)}) custom-call(bf16[1,768,256]{2,1,0:T(8,128)(2,1)} %x_in.1, f32[3,2,768]{2,1,0:T(2,128)} %bitcast.2, s32[2]{0:T(128)} %dil_in.1, s32[1,64]{1,0:T(1,128)} %link_in.1, bf16[112,768]{1,0:T(8,128)(2,1)} %proj_in.1, bf16[1,14,8192]{2,1,0:T(8,128)(2,1)} %cot_in.1), custom_call_target="tpu_custom_call" | custom-call | flops 1000000000 | bytes 4000000 | tf_op jit(solution)/shard_map/pallas_call | solution.py:559
  48.8 0.8 %shard_map.86 = (bf16[1,768,256]{2,1,0:T(8,128)(2,1)}, f32[14,768]{1,0:T(8,128)}, f32[3,2,768]{2,1,0:T(2,128)}) custom-call(bf16[1,768,256]{2,1,0:T(8,128)(2,1)S(1)} %get-tuple-element.9.refs_0_, f32[14,768]{1,0:T(8,128)S(1)} %get-tuple-element.10.refs_1_, f32[3,2,768]{2,1,0:T(2,128)S(1)} %get-tuple-element.11.refs_2_), custom_call_target="tpu_custom_call" | custom-call | tf_op jit(solution)/shard_map/pallas_call | solution.py:575

commit v5 on v4

--- a/solution.py
+++ b/solution.py
@@ -21,7 +21,7 @@
 PAD = 16
 SLAB = 64
 LAST_DILATION = 8
-Z_PART, X_PART, SIB_PART = 32, 36, 40
+Z_PART, X_PART, SIB_PART, A_X, A_Y = 32, 36, 40, 44, 46
 FAR_FIRST = sorted(
     range(1, SEQ),
     key=lambda m: -100 * (m & 1) - ((0, 1, 2, 2)[m >> 4] + (0, 1, 2, 2, 4, 3, 2, 2)[(m >> 1) & 7]),
@@ -59,7 +59,7 @@
     stage, cot, cot_sib, pfull, edge_s, edge_r, cot_t, halo, wide,
     a0, a1, s0, s1, x2, pooled, pooled_sib, g2, g1, moved, prods, unit, halves, spread, matrix1, matrix0, pick_taps,
     a_s1, a_r1, a_s2, a_r2, a_s3, a_r3, a_r4, b_s1, b_r1, b_s2, b_r2, b_r3,
-    t_r1, t_r2, t_r3,
+    t_r1, t_r2, t_r3, t_f,
     send, recv, load,
 ):
     s = lax.axis_index("seq")
@@ -86,12 +86,15 @@
 
     whole = {
         0: edge_s.at[0], 1: edge_s.at[0], 2: stage.at[pl.ds(0, 32)], 6: stage.at[pl.ds(0, 31)], 7: pooled, 12: cot_sib,
-        13: b_r1.at[pl.ds(0, 7)], 14: a_r1.at[pl.ds(0, 3)], 21: cot_t.at[pl.ds(0, PAD)], 22: cot_t.at[pl.ds(0, PAD)],
-        23: t_r1.at[pl.ds(0, 7)], 24: b_r2.at[pl.ds(0, 7)], 25: a_r2.at[pl.ds(0, 7)], 28: a_r3.at[pl.ds(0, 7)],
+        13: b_r1.at[pl.ds(0, 7)], 21: cot_t.at[pl.ds(0, PAD)], 22: cot_t.at[pl.ds(0, PAD)],
+        23: t_r1.at[pl.ds(0, 7)], 24: b_r2.at[pl.ds(0, 7)], 28: a_r3.at[pl.ds(0, 7)],
         26: t_r2.at[pl.ds(0, 7)], 27: b_r3.at[pl.ds(0, 3)],
-        29: t_r3.at[pl.ds(0, 7)], 30: a_r4.at[pl.ds(0, 3)],
+        29: t_r3.at[pl.ds(0, 7)], 31: t_f, 30: a_r4.at[pl.ds(0, 3)],
         3: pfull.at[0, pl.ds(0, 3)], 4: pfull.at[0, pl.ds(0, 4)],
     }
+    for h in range(2):
+        whole[A_X + h] = a_r1.at[pl.ds(0, 3), pl.ds(0, 2)]
+        whole[A_Y + h] = a_r2.at[pl.ds(0, 7), pl.ds(0, 2)]
     for i in range(4):
         whole[Z_PART + i] = pfull.at[0, 0, pl.ds(0, PAD)]
         whole[X_PART + i] = pfull.at[0, pl.ds(0, 3), pl.ds(0, PAD)]
@@ -118,11 +121,27 @@
         ended.append(i)
         dummy(i).wait_recv()
 
+    def on_core(c):
+        return pl.when(core == c)
+
     def finish():
         for i in started:
             if i not in ended:
                 arrived(i)
-            if i in range(Z_PART, Z_PART + 4):
+            if i == 23:
+                for c in range(2):
+                    @on_core(c)
+                    def _():
+                        block = t_r1.at[pl.ds(0, 4 - c)]
+                        pltpu.make_async_remote_copy(
+                            src_ref=block, dst_ref=block, send_sem=send.at[i], recv_sem=recv.at[i],
+                            device_id=sibling, device_id_type=MESH,
+                        ).wait_send()
+            elif i in (26, 29, 31):
+                @on_core(1)
+                def _():
+                    dummy(i).wait_send()
+            elif i in range(Z_PART, Z_PART + 4):
                 @pl.when((zl == 0) | (zl == 3))
                 def _():
                     dummy(i).wait_send()
@@ -353,10 +372,26 @@
             a_s1[2 * j] = part[:, :HALF].reshape(4, 8, PAD, HALF)
             a_s1[2 * j + 1] = part[:, HALF:].reshape(4, 8, PAD, HALF)
         if j == 1:
-            for k in (2, 1, 3):
-                push(a_s1.at[(x + k) % 4], a_r1.at[x], 14, at_x(k))
+            for h in range(2):
+                part_z = pl.ds(2 * h, 2)
+                for k in (2, 1, 3):
+                    push(a_s1.at[(x + k) % 4, part_z], a_r1.at[x, part_z], A_X + h, at_x(k))
     b_r1[y] = b_s1[:, y]
     a_r1[x] = a_s1[x]
+
+    def total(ref):
+        parts = [ref[i].astype(F32) for i in range(ref.shape[0])]
+        while len(parts) > 1:
+            parts = [a + b for a, b in zip(parts[::2], parts[1::2])]
+        return parts[0]
+
+    def weight_y(h):
+        part_z = pl.ds(2 * h, 2)
+        arrived(A_X + h)
+        a_s2[part_z] = total(a_r1.at[:, part_z]).astype(BF)
+        for k in FAR_RING:
+            yy = (y + k) % 8
+            push(a_s2.at[part_z, yy], a_r2.at[y, part_z], A_Y + h, at_y(yy))
 
     arrived(3)
     rows = pfull.at[core, pl.ds(zh * 4, 4)]
@@ -395,6 +430,7 @@
         for k, part in enumerate((hi, g, lo)):
             keep_product(rows, 2 * k + 1, a1[0, rows, :] * part[0] + a1[1, rows, :] * part[1])
 
+    weight_y(0)
     moved[:, :2 * ROWS] = jnp.dot(g1[...], matrix0[...], preferred_element_type=F32)
 
     def around(rows):
@@ -412,11 +448,27 @@
     flat = lax.dot_general(pick_taps[...], prods[...], nt, preferred_element_type=F32)
     slot = x * 2 + core
     t_r1[slot] = jnp.concatenate([flat[:, :384], flat[:, 384:]], axis=0).astype(BF)
-    for k in (2, 1, 3, 0):
-        for cc in range(2):
-            if k:
-                push(t_r1.at[slot], t_r1.at[slot], 23, at_x_core((x + k) % 4, cc))
-    push(t_r1.at[slot], t_r1.at[slot], 23, sibling)
+    for k in (2, 1, 3):
+        push(t_r1.at[slot], t_r1.at[slot], 23, at_x_core((x + k) % 4, 1))
+
+    @on_core(0)
+    def _():
+        push(t_r1.at[slot], t_r1.at[slot], 23, sibling)
+
+    def push_unless(zz, src):
+        @pl.when(zz != z8)
+        def _():
+            push(src, a_r3.at[z8], 28, at_z(zz))
+
+    weight_y(1)
+    a_r2[y] = a_s2[:, y]
+
+    arrived(13)
+    b_s2[...] = total(b_r1).astype(BF)
+    for k in FAR_RING:
+        zz = (z8 + k) % 8
+        push(b_s2.at[zz % 4], b_r2.at[z8], 24, at_z(zz))
+    b_r2[z8] = b_s2[zl]
 
     @pl.loop(0, C // SLAB)
     def _(i):
@@ -427,36 +479,20 @@
             conv = (w[0] * hi[j] + w[1] * g[j]) + w[2] * lo[j]
             out_ref[0, rows, HALF * j:HALF * (j + 1)] = (g[j] + conv * s0[j, rows, :]).astype(BF)
 
-    def total(ref):
-        parts = [ref[i].astype(F32) for i in range(ref.shape[0])]
-        while len(parts) > 1:
-            parts = [a + b for a, b in zip(parts[::2], parts[1::2])]
-        return parts[0]
-
-    arrived(14)
-    a_s2[...] = total(a_r1).astype(BF)
-    for k in FAR_RING:
-        yy = (y + k) % 8
-        push(a_s2.at[:, yy], a_r2.at[y], 25, at_y(yy))
-    a_r2[y] = a_s2[:, y]
-
-    arrived(13)
-    b_s2[...] = total(b_r1).astype(BF)
-    for k in FAR_RING:
-        zz = (z8 + k) % 8
-        push(b_s2.at[zz % 4], b_r2.at[z8], 24, at_z(zz))
-    b_r2[z8] = b_s2[zl]
-
-    arrived(23)
-    t_r2[z8] = total(t_r1).astype(BF)
-    for k in FAR_RING:
-        push(t_r2.at[z8], t_r2.at[z8], 26, at_z((z8 + k) % 8))
-
-    arrived(25)
-    a_s3[...] = total(a_r2).astype(BF)
-    for k in FAR_RING:
-        zz = (z8 + k) % 8
-        push(a_s3.at[zz % 4], a_r3.at[z8], 28, at_z(zz))
+    @on_core(1)
+    def _():
+        arrived(23)
+        t_r2[z8] = total(t_r1).astype(BF)
+        for k in FAR_RING:
+            push(t_r2.at[z8], t_r2.at[z8], 26, at_z((z8 + k) % 8))
+
+    for h in range(2):
+        part_z = pl.ds(2 * h, 2)
+        arrived(A_Y + h)
+        a_s3[part_z] = total(a_r2.at[:, part_z]).astype(BF)
+        for low in (2 * h, 2 * h + 1):
+            for high in (0, 4):
+                push_unless(high + low, a_s3.at[low])
     a_r3[z8] = a_s3[zl]
 
     arrived(24)
@@ -464,18 +500,23 @@
     for k in (1, 3, 2):
         push(b_r3.at[x], b_r3.at[x], 27, at_x(k))
 
-    arrived(26)
-    t_r3[y] = total(t_r2).astype(BF)
-    for k in FAR_RING:
-        push(t_r3.at[y], t_r3.at[y], 29, at_y((y + k) % 8))
+    @on_core(1)
+    def _():
+        arrived(26)
+        t_r3[y] = total(t_r2).astype(BF)
+        for k in FAR_RING:
+            push(t_r3.at[y], t_r3.at[y], 29, at_y((y + k) % 8))
 
     arrived(28)
     a_r4[x] = total(a_r3)
     for k in (2, 1, 3):
         push(a_r4.at[x], a_r4.at[x], 30, at_x(k))
 
-    arrived(29)
-    taps_total = total(t_r3)
+    @on_core(1)
+    def _():
+        arrived(29)
+        t_f[...] = total(t_r3)
+        push(t_f, t_f, 31, sibling)
 
     scale = 1.0 / math.sqrt(SEQ * DP * HALF)
     arrived(27)
@@ -483,6 +524,11 @@
     arrived(30)
     for j in range(4):
         pg_ref[:, HALF * j:HALF * (j + 1)] = a_r4[j][:OWN] * scale
+    @on_core(0)
+    def _():
+        arrived(31)
+
+    taps_total = t_f[...]
     for h in range(2):
         for k in range(3):
             tg_ref[k, :, 384 * h:384 * (h + 1)] = taps_total[8 * h + 2 * k:8 * h + 2 * k + 2] * scale
@@ -545,6 +591,7 @@
     ((8, PAD, 384), BF),
     ((8, PAD, 384), BF),
     ((8, PAD, 384), BF),
+    ((PAD, 384), F32),
 ]
 
 
@@ -564,7 +611,7 @@
         scratch_shapes=[pltpu.VMEM(shape, kind) for shape, kind in SCRATCH[:4]]
         + [pltpu.SMEM((2,), jnp.int32), pltpu.SMEM((1, SEQ), jnp.int32)]
         + [pltpu.VMEM(shape, kind) for shape, kind in SCRATCH[4:]]
-        + [pltpu.SemaphoreType.DMA((44,)), pltpu.SemaphoreType.DMA((44,)), pltpu.SemaphoreType.DMA((6,))],
+        + [pltpu.SemaphoreType.DMA((48,)), pltpu.SemaphoreType.DMA((48,)), pltpu.SemaphoreType.DMA((6,))],
         compiler_params=pltpu.CompilerParams(
             collective_id=0, has_side_effects=True, vmem_limit_bytes=60 * 1024 * 1024
         ),

time: 49.7 us -> 49.8 us (level)
  no operation moved by 1% of the time
where the time goes in v5:
time: 49.8 us; the launch traced here: 49.7 us
  Pallas kernels  49 us (98%)
  between operations  0.64 us (1%)
    pallas_call x1, Pallas kernels, local(): pl.pallas_call(kernel, out_shape=tuple((pltpu.VMEM(r.shape, r.dtype) for...  48.2 us

profile of v5, /device:TPU:1, one launch (start us, length us, event | category | flops | bytes accessed | tf_op | source)
XLA Modules:
  0.0 49.7 jit_solution(4339892223023668870)
XLA Ops:
  0.6 48.2 %shard_map.85 = (bf16[1,768,256]{2,1,0:T(8,128)(2,1)S(1)}, f32[14,768]{1,0:T(8,128)S(1)}, f32[3,2,768]{2,1,0:T(2,128)S(1)}) custom-call(bf16[1,768,256]{2,1,0:T(8,128)(2,1)} %x_in.1, f32[3,2,768]{2,1,0:T(2,128)} %bitcast.2, s32[2]{0:T(128)} %dil_in.1, s32[1,64]{1,0:T(1,128)} %link_in.1, bf16[112,768]{1,0:T(8,128)(2,1)} %proj_in.1, bf16[1,14,8192]{2,1,0:T(8,128)(2,1)} %cot_in.1), custom_call_target="tpu_custom_call" | custom-call | flops 1000000000 | bytes 4000000 | tf_op jit(solution)/shard_map/pallas_call | solution.py:606
  48.9 0.8 %shard_map.86 = (bf16[1,768,256]{2,1,0:T(8,128)(2,1)}, f32[14,768]{1,0:T(8,128)}, f32[3,2,768]{2,1,0:T(2,128)}) custom-call(bf16[1,768,256]{2,1,0:T(8,128)(2,1)S(1)} %get-tuple-element.9.refs_0_, f32[14,768]{1,0:T(8,128)S(1)} %get-tuple-element.10.refs_1_, f32[3,2,768]{2,1,0:T(2,128)S(1)} %get-tuple-element.11.refs_2_), custom_call_target="tpu_custom_call" | custom-call | tf_op jit(solution)/shard_map/pallas_call | solution.py:622

commit v6 on v5

--- a/solution.py
+++ b/solution.py
@@ -53,9 +53,9 @@
 
 
 def kernel(
-    x_in, taps_in, dil_in, link_in, proj_in, cot_in,
+    x_ref, taps_in, dil_in, link_in, proj_ref, cot_ref,
     out_ref, pg_ref, tg_ref,
-    x_ref, taps_ref, proj_ref, cot_ref, dil_ref, link_ref,
+    taps_ref, dil_ref, link_ref,
     stage, cot, cot_sib, pfull, edge_s, edge_r, cot_t, halo, wide,
     a0, a1, s0, s1, x2, pooled, pooled_sib, g2, g1, moved, prods, unit, halves, spread, matrix1, matrix0, pick_taps,
     a_s1, a_r1, a_s2, a_r2, a_s3, a_r3, a_r4, b_s1, b_r1, b_s2, b_r2, b_r3,
@@ -153,7 +153,7 @@
         pltpu.make_async_copy(a, b, load.at[i])
         for i, (a, b) in enumerate(
             (
-                (cot_in, cot_ref), (x_in, x_ref), (proj_in, proj_ref), (taps_in, taps_ref),
+                (taps_in, taps_ref),
                 (dil_in, dil_ref), (link_in, link_ref),
             )
         )
@@ -201,17 +201,14 @@
             tile = jnp.where(lane < HALF // 2, right, left)
             dst[pl.ds(96 * k, 96), :] = jnp.where(halo_keep(16), tile, 0.0)
 
-    loads[0].wait()
     for t in range(SEQ):
         block = cot_ref[0, :, pl.ds(HALF * t, HALF)]
         stage[t] = jnp.concatenate(
             [block.astype(F32), jnp.zeros((PAD - OWN, HALF), F32)], axis=0
         ).astype(BF)
 
-    loads[1].wait()
     pack_edges(lambda j, rows: x_ref[0, rows, pl.ds(HALF * j, HALF)], edge_s)
 
-    loads[2].wait()
     row = lax.broadcasted_iota(jnp.int32, (64, 112), 0)
     col = lax.broadcasted_iota(jnp.int32, (64, 112), 1)
     inner = row % PAD
@@ -219,7 +216,7 @@
     pick = jnp.where((inner < OWN) & (source == col), 1.0, 0.0).astype(BF)
     pfull[core, d] = jnp.dot(pick, proj_ref[...], preferred_element_type=F32).astype(BF)
 
-    for copy in loads[3:]:
+    for copy in loads:
         copy.wait()
     left_linked = link_ref[0, s] >= 0
     right_linked = link_ref[0, (s + 1) % SEQ] >= 0
@@ -546,10 +543,7 @@
 
 
 SCRATCH = [
-    ((1, C, ROWS), BF),
     ((3, 2, C), F32),
-    ((112, C), BF),
-    ((1, OWN, SEQ * HALF), BF),
     ((SEQ, PAD, HALF), BF),
     ((SEQ, PAD, HALF), BF),
     ((32, PAD, HALF), BF),
@@ -606,11 +600,11 @@
     parts = pl.pallas_call(
         kernel,
         out_shape=tuple(pltpu.VMEM(r.shape, r.dtype) for r in results),
-        in_specs=[hbm] * 6,
+        in_specs=[vmem, hbm, hbm, hbm, vmem, vmem],
         out_specs=(vmem,) * 3,
-        scratch_shapes=[pltpu.VMEM(shape, kind) for shape, kind in SCRATCH[:4]]
+        scratch_shapes=[pltpu.VMEM(shape, kind) for shape, kind in SCRATCH[:1]]
         + [pltpu.SMEM((2,), jnp.int32), pltpu.SMEM((1, SEQ), jnp.int32)]
-        + [pltpu.VMEM(shape, kind) for shape, kind in SCRATCH[4:]]
+        + [pltpu.VMEM(shape, kind) for shape, kind in SCRATCH[1:]]
         + [pltpu.SemaphoreType.DMA((48,)), pltpu.SemaphoreType.DMA((48,)), pltpu.SemaphoreType.DMA((6,))],
         compiler_params=pltpu.CompilerParams(
             collective_id=0, has_side_effects=True, vmem_limit_bytes=60 * 1024 * 1024

time: 49.8 us -> 50.6 us (1.016)
  Pallas kernels: 49 us -> 49.8 us
    pallas_call x1, Pallas kernels: 48.2 us -> 49 us  [local(): pl.pallas_call(kernel, out_shape=tuple((pltpu.VMEM(r.shape, r.dtype) for...]
where the time goes in v6:
time: 50.6 us; the launch traced here: 50.4 us
  Pallas kernels  49.8 us (98%)
  between operations  0.64 us (1%)
    pallas_call x1, Pallas kernels, local(): pl.pallas_call(kernel, out_shape=tuple((pltpu.VMEM(r.shape, r.dtype) for...  49 us

profile of v6, /device:TPU:1, one launch (start us, length us, event | category | flops | bytes accessed | tf_op | source)
XLA Modules:
  0.0 50.4 jit_solution(14113573302816433806)
XLA Ops:
  0.6 49.0 %shard_map.85 = (bf16[1,768,256]{2,1,0:T(8,128)(2,1)S(1)}, f32[14,768]{1,0:T(8,128)S(1)}, f32[3,2,768]{2,1,0:T(2,128)S(1)}) custom-call(bf16[1,768,256]{2,1,0:T(8,128)(2,1)} %x_ref.1, f32[3,2,768]{2,1,0:T(2,128)} %bitcast.2, s32[2]{0:T(128)} %dil_in.1, s32[1,64]{1,0:T(1,128)} %link_in.1, bf16[112,768]{1,0:T(8,128)(2,1)} %proj_ref.1, bf16[1,14,8192]{2,1,0:T(8,128)(2,1)} %cot_ref.1), custom_call_target="tpu_custom_call" | custom-call | flops 1000000000 | bytes 4000000 | tf_op jit(solution)/shard_map/pallas_call | solution.py:600
  49.7 0.8 %shard_map.86 = (bf16[1,768,256]{2,1,0:T(8,128)(2,1)}, f32[14,768]{1,0:T(8,128)}, f32[3,2,768]{2,1,0:T(2,128)}) custom-call(bf16[1,768,256]{2,1,0:T(8,128)(2,1)S(1)} %get-tuple-element.9.refs_0_, f32[14,768]{1,0:T(8,128)S(1)} %get-tuple-element.10.refs_1_, f32[3,2,768]{2,1,0:T(2,128)S(1)} %get-tuple-element.11.refs_2_), custom_call_target="tpu_custom_call" | custom-call | tf_op jit(solution)/shard_map/pallas_call | solution.py:616
